TPU v7x, 32 devices: a whole 2x2x4 slice. The times are simulated.
32 devices in a mesh: seq: 4 (over y, x), dp: 8 (over z, core).
Axes of the slice: x: 2, y: 2, z: 4, core: 2. Of those that a mesh axis runs over, the one named last changes fastest.
Arguments:
- tokens: bfloat16 [8, 1024, 1152], P('dp', 'seq'), may hold values from -6 to 6
- cotangent: bfloat16 [8, 1024, 1152], P('dp', 'seq'), may hold values from -6 to 6
- picture_starts: int32 [8, 2], P('dp'), may hold values from 0 to 768, as said below
- query_weight: float32 [1152, 1152], P('seq'), may hold values from -0.1875 to 0.1875
- key_matrix: float32 [1152, 384], P('seq'), may hold values from -0.1875 to 0.1875
- value_matrix: float32 [1152, 384], P('seq'), may hold values from -0.1875 to 0.1875
- out_weight: float32 [1152, 1152], P('seq'), may hold values from -2.5 to 2.5
- gate_weight: float32 [1152, 3072], P('seq'), may hold values from -0.1875 to 0.1875
- up_weight: float32 [1152, 3072], P('seq'), may hold values from -0.1875 to 0.1875
- down_weight: float32 [3072, 1152], P('seq'), may hold values from -0.109375 to 0.109375
- attention_gain: float32 [1152], P('seq'), may hold values from 0.3 to 2.5
- feed_gain: float32 [1152], P('seq'), may hold values from 0.3 to 2.5
- query_moment: float32 [1152, 1152], P('seq'), may hold values from -6 to 6
- key_velocity: float32 [1152, 384], P('seq'), may hold values from -6 to 6
- value_velocity: float32 [1152, 384], P('seq'), may hold values from -6 to 6
- out_moment: float32 [1152, 1152], P('seq'), may hold values from -6 to 6
- gate_moment: float32 [1152, 3072], P('seq'), may hold values from -6 to 6
- up_moment: float32 [1152, 3072], P('seq'), may hold values from -6 to 6
- down_moment: float32 [3072, 1152], P('seq'), may hold values from -6 to 6
- attention_moment: float32 [1152], P('seq'), may hold values from -6 to 6
- feed_moment: float32 [1152], P('seq'), may hold values from -6 to 6
Outputs:
- layer_output: bfloat16 [8, 1024, 1152], P('dp', 'seq')
- input_gradient: float32 [8, 1024, 1152], P('dp', 'seq')
- query_momentum: float32 [1152, 1152], P('seq')
- key_momentum: float32 [1152, 384], P('seq')
- value_momentum: float32 [1152, 384], P('seq')
- out_momentum: float32 [1152, 1152], P('seq')
- gate_momentum: float32 [1152, 3072], P('seq')
- up_momentum: float32 [1152, 3072], P('seq')
- down_momentum: float32 [3072, 1152], P('seq')
- attention_momentum: float32 [1152], P('seq')
- feed_momentum: float32 [1152], P('seq')
- query_updated: float32 [1152, 1152], P('seq')
- key_updated: float32 [1152, 384], P('seq')
- value_updated: float32 [1152, 384], P('seq')
- out_updated: float32 [1152, 1152], P('seq')
- gate_updated: float32 [1152, 3072], P('seq')
- up_updated: float32 [1152, 3072], P('seq')
- down_updated: float32 [3072, 1152], P('seq')
- attention_updated: float32 [1152], P('seq')
- feed_updated: float32 [1152], P('seq')
- gradient_norm: float32 [], replicated
Inputs may be any that keep to these rules, and one draw needn't show every extreme that they name: `picture_starts`: row s holds the first positions of the 2 picture pieces of sequence s, each 256 positions long; piece p lies within positions p * 512 to (p + 1) * 512 - 1, so pieces ascend and never meet.
All inputs are finite; a program needn't handle non-finite values.
Results may differ from a plain program's by a relative error of at most 0.015.
Values may be sent and summed in bfloat16 or wider, within the bound.
No kernel may reach another device: no remote copies, remote signals or barrier semaphores. Data moves between devices by JAX's collectives and lax.ppermute only.
A program may use at most 256 MiB of HBM per device.

v0:
```python
from functools import partial
import math

import jax
import jax.numpy as jnp
from jax import lax
from jax.sharding import PartitionSpec as P

QUERY_HEAD_COUNT = 18
KEY_VALUE_HEADS = 6
HEAD_SIZE = 64
PIECE = 256
PARAMS = 14158080


learning_rate = 0.25
weight_decay = 0.1
momentum_beta = 0.5


def rms_scale(values, scaling):
    return values * lax.rsqrt(jnp.mean(values * values, axis=-1, keepdims=True) + 1e-05) * scaling


def apply_rotary(values, token_positions):
    half_width = values.shape[-1] // 2
    frequency = 10000.0 ** (-jnp.arange(half_width, dtype=jnp.float32) / half_width)
    angles = token_positions.astype(jnp.float32)[:, None] * frequency[None, :]
    cosine = jnp.cos(angles)[:, None, :]
    sine_part = jnp.sin(angles)[:, None, :]
    leading = values[..., :half_width]
    trailing = values[..., half_width:]
    return jnp.concatenate(
        [leading * cosine - trailing * sine_part, trailing * cosine + leading * sine_part], axis=-1
    )


def swiglu(gate_values, up_values):
    return jax.nn.silu(gate_values) * up_values


def piece_number(token_positions, starts):
    inside = (token_positions[:, None] >= starts[None, :]) & (
        token_positions[:, None] < starts[None, :] + PIECE
    )
    numbers = jnp.arange(starts.shape[0], dtype=jnp.int32) + 1
    return jnp.sum(jnp.where(inside, numbers[None, :], 0), axis=1) - 1


def visible(query_position, query_piece, key_position, key_piece):
    earlier = key_position[None, :] <= query_position[:, None]
    same_piece = (query_piece[:, None] == key_piece[None, :]) & (query_piece[:, None] >= 0)
    return earlier | same_piece


def per_device(
    tokens,
    cotangent,
    picture_starts,
    query_weight,
    key_matrix,
    value_matrix,
    out_weight,
    gate_weight,
    up_weight,
    down_weight,
    attention_gain,
    feed_gain,
    query_moment,
    key_velocity,
    value_velocity,
    out_moment,
    gate_moment,
    up_moment,
    down_moment,
    attention_moment,
    feed_moment,
):
    masters = (
        query_weight,
        key_matrix,
        value_matrix,
        out_weight,
        gate_weight,
        up_weight,
        down_weight,
        attention_gain,
        feed_gain,
    )
    moments = (
        query_moment,
        key_velocity,
        value_velocity,
        out_moment,
        gate_moment,
        up_moment,
        down_moment,
        attention_moment,
        feed_moment,
    )
    shard_query = query_weight.astype(jnp.bfloat16)
    shard_key = key_matrix.astype(jnp.bfloat16)
    shard_value = value_matrix.astype(jnp.bfloat16)
    shard_out = out_weight.astype(jnp.bfloat16)
    shard_gate = gate_weight.astype(jnp.bfloat16)
    shard_up = up_weight.astype(jnp.bfloat16)
    shard_down = down_weight.astype(jnp.bfloat16)
    shard_gain_one = attention_gain.astype(jnp.bfloat16)
    shard_gain_two = feed_gain.astype(jnp.bfloat16)
    gathered = (
        lax.all_gather(shard_query, "seq", axis=0, tiled=True),
        lax.all_gather(shard_key, "seq", axis=0, tiled=True),
        lax.all_gather(shard_value, "seq", axis=0, tiled=True),
        lax.all_gather(shard_out, "seq", axis=0, tiled=True),
        lax.all_gather(shard_gate, "seq", axis=0, tiled=True),
        lax.all_gather(shard_up, "seq", axis=0, tiled=True),
        lax.all_gather(shard_down, "seq", axis=0, tiled=True),
        lax.all_gather(shard_gain_one, "seq", axis=0, tiled=True),
        lax.all_gather(shard_gain_two, "seq", axis=0, tiled=True),
    )
    full_query, complete_key, complete_value, full_out, full_gate, full_up, full_down = gathered[:7]
    gain_one = gathered[7].astype(jnp.float32)
    gain_two = gathered[8].astype(jnp.float32)
    group_size = lax.axis_size("seq")
    local_rows = tokens.shape[1]
    sequence_length = local_rows * group_size
    heads_per_group = QUERY_HEAD_COUNT // KEY_VALUE_HEADS
    token_positions = lax.axis_index("seq") * local_rows + jnp.arange(local_rows, dtype=jnp.int32)
    starts = picture_starts[0]
    query_piece = piece_number(token_positions, starts)
    key_positions = jnp.arange(sequence_length, dtype=jnp.int32)
    key_pieces = piece_number(key_positions, starts)
    layer_input = tokens[0].astype(jnp.float32)
    normed_one, pull_norm_one = jax.vjp(rms_scale, layer_input, gain_one)
    first_activation = normed_one.astype(jnp.bfloat16)
    rotation = partial(apply_rotary, token_positions=token_positions)
    query_linear = jnp.dot(
        first_activation, full_query, preferred_element_type=jnp.float32
    ).reshape(local_rows, QUERY_HEAD_COUNT, HEAD_SIZE)
    rotated_query, pull_query = jax.vjp(rotation, query_linear)
    query_reduced = rotated_query.astype(jnp.bfloat16).reshape(
        local_rows, KEY_VALUE_HEADS, heads_per_group, HEAD_SIZE
    )
    key_linear = jnp.dot(
        first_activation, complete_key, preferred_element_type=jnp.float32
    ).reshape(local_rows, KEY_VALUE_HEADS, HEAD_SIZE)
    rotated_key, key_pullback = jax.vjp(rotation, key_linear)
    key_reduced = rotated_key.astype(jnp.bfloat16).reshape(local_rows, KEY_VALUE_HEADS * HEAD_SIZE)
    value_reduced = jnp.dot(
        first_activation, complete_value, preferred_element_type=jnp.float32
    ).astype(jnp.bfloat16)
    every_key_row, every_value_row = (
        lax.all_gather(key_reduced, "seq", axis=0, tiled=True),
        lax.all_gather(value_reduced, "seq", axis=0, tiled=True),
    )
    every_key_row = every_key_row.reshape(sequence_length, KEY_VALUE_HEADS, HEAD_SIZE)
    every_value_row = every_value_row.reshape(sequence_length, KEY_VALUE_HEADS, HEAD_SIZE)
    rows_per_block = math.gcd(512, sequence_length)
    count_of_blocks = sequence_length // rows_per_block
    last_position = token_positions[local_rows - 1]
    last_piece = query_piece[local_rows - 1]

    def needed(number):
        first_row = number * rows_per_block
        return (first_row <= last_position) | (last_piece >= 0) & (
            key_pieces[first_row] == last_piece
        )

    def block_scores(number):
        first_row = number * rows_per_block
        key_block = lax.dynamic_slice_in_dim(every_key_row, first_row, rows_per_block, 0)
        value_block = lax.dynamic_slice_in_dim(every_value_row, first_row, rows_per_block, 0)
        allowed = visible(
            token_positions,
            query_piece,
            lax.dynamic_slice_in_dim(key_positions, first_row, rows_per_block, 0),
            lax.dynamic_slice_in_dim(key_pieces, first_row, rows_per_block, 0),
        )
        raw_scores = jnp.einsum(
            "qhgd,khd->hgqk", query_reduced, key_block, preferred_element_type=jnp.float32
        )
        exponent = jnp.where(allowed[None, None], jnp.exp(raw_scores * 0.125), 0.0)
        return (key_block, value_block, exponent)

    def unchanged(current):
        return current

    def forward_step(number, running):

        def forward_compute(current):
            summed, totals = current
            key_block, value_block, exponent = block_scores(number)
            summed = summed + jnp.einsum(
                "hgqk,khd->hgqd",
                exponent.astype(jnp.bfloat16),
                value_block,
                preferred_element_type=jnp.float32,
            )
            return (summed, totals + jnp.sum(exponent, axis=-1))

        return lax.cond(needed(number), forward_compute, unchanged, running)

    initial_sum = jnp.zeros((KEY_VALUE_HEADS, heads_per_group, local_rows, HEAD_SIZE), jnp.float32)
    initial_total = jnp.zeros((KEY_VALUE_HEADS, heads_per_group, local_rows), jnp.float32)
    summed, totals = lax.fori_loop(0, count_of_blocks, forward_step, (initial_sum, initial_total))
    attended = summed / totals[..., None]
    attention = (
        jnp.transpose(attended, (2, 0, 1, 3))
        .reshape(local_rows, QUERY_HEAD_COUNT * HEAD_SIZE)
        .astype(jnp.bfloat16)
    )
    residual = layer_input + jnp.dot(attention, full_out, preferred_element_type=jnp.float32)
    normed_two, pull_norm_two = jax.vjp(rms_scale, residual, gain_two)
    act_two = normed_two.astype(jnp.bfloat16)
    gate_linear = jnp.dot(act_two, full_gate, preferred_element_type=jnp.float32)
    up_linear = jnp.dot(act_two, full_up, preferred_element_type=jnp.float32)
    hidden_full, pull_swiglu = jax.vjp(swiglu, gate_linear, up_linear)
    hidden = hidden_full.astype(jnp.bfloat16)
    layer_out = residual + jnp.dot(hidden, full_down, preferred_element_type=jnp.float32)
    output = layer_out.astype(jnp.bfloat16)[None]
    upstream = cotangent[0].astype(jnp.float32)
    upstream_low = upstream.astype(jnp.bfloat16)
    grad_down = jnp.einsum("nf,nd->fd", hidden, upstream_low, preferred_element_type=jnp.float32)
    grad_hidden = jnp.einsum(
        "nd,fd->nf", upstream_low, full_down, preferred_element_type=jnp.float32
    )
    grad_gate_full, grad_up_full = pull_swiglu(grad_hidden)
    gate_back = grad_gate_full.astype(jnp.bfloat16)
    up_back = grad_up_full.astype(jnp.bfloat16)
    grad_gate = jnp.einsum("nd,nf->df", act_two, gate_back, preferred_element_type=jnp.float32)
    grad_up = jnp.einsum("nd,nf->df", act_two, up_back, preferred_element_type=jnp.float32)
    grad_act_two = jnp.einsum(
        "nf,df->nd", gate_back, full_gate, preferred_element_type=jnp.float32
    ) + jnp.einsum("nf,df->nd", up_back, full_up, preferred_element_type=jnp.float32)
    residual_norm_grad, grad_gain_two = pull_norm_two(grad_act_two)
    grad_residual = upstream + residual_norm_grad
    residual_back = grad_residual.astype(jnp.bfloat16)
    grad_out = jnp.einsum("nk,nd->kd", attention, residual_back, preferred_element_type=jnp.float32)
    attention_pullback = jnp.einsum(
        "nd,kd->nk", residual_back, full_out, preferred_element_type=jnp.float32
    ).astype(jnp.bfloat16)
    attention_pullback = jnp.transpose(
        attention_pullback.reshape(local_rows, KEY_VALUE_HEADS, heads_per_group, HEAD_SIZE),
        (1, 2, 0, 3),
    )
    back_full = attention_pullback.astype(jnp.float32)
    scaled_back = (back_full / totals[..., None]).astype(jnp.bfloat16)
    total_back = -jnp.sum(back_full * attended, axis=-1) / totals
    query_heads = jnp.transpose(query_reduced, (1, 2, 0, 3))

    def backward_step(number, running):

        def backward_compute(current):
            grad_query_sum, key_gradient_rows, value_gradient_rows = current
            first_row = number * rows_per_block
            key_block, value_block, exponent = block_scores(number)
            through = jnp.einsum(
                "hgqd,khd->hgqk", scaled_back, value_block, preferred_element_type=jnp.float32
            )
            score_back = (exponent * (through + total_back[..., None])).astype(jnp.bfloat16)
            grad_query_sum = (
                grad_query_sum
                + jnp.einsum(
                    "hgqk,khd->hgqd", score_back, key_block, preferred_element_type=jnp.float32
                )
                * 0.125
            )
            key_part = (
                jnp.einsum(
                    "hgqk,hgqd->khd", score_back, query_heads, preferred_element_type=jnp.float32
                )
                * 0.125
            )
            value_part = jnp.einsum(
                "hgqk,hgqd->khd",
                exponent.astype(jnp.bfloat16),
                scaled_back,
                preferred_element_type=jnp.float32,
            )
            key_gradient_rows = lax.dynamic_update_slice_in_dim(
                key_gradient_rows, key_part, first_row, 0
            )
            value_gradient_rows = lax.dynamic_update_slice_in_dim(
                value_gradient_rows, value_part, first_row, 0
            )
            return (grad_query_sum, key_gradient_rows, value_gradient_rows)

        return lax.cond(needed(number), backward_compute, unchanged, running)

    initial_query = jnp.zeros(
        (KEY_VALUE_HEADS, heads_per_group, local_rows, HEAD_SIZE), jnp.float32
    )
    initial_keys = jnp.zeros((sequence_length, KEY_VALUE_HEADS, HEAD_SIZE), jnp.float32)
    grad_query_sum, key_gradient_rows, value_gradient_rows = lax.fori_loop(
        0, count_of_blocks, backward_step, (initial_query, initial_keys, initial_keys)
    )
    local_key_rows, value_own = (
        lax.psum_scatter(
            key_gradient_rows.reshape(sequence_length, KEY_VALUE_HEADS * HEAD_SIZE),
            "seq",
            scatter_dimension=0,
            tiled=True,
        ),
        lax.psum_scatter(
            value_gradient_rows.reshape(sequence_length, KEY_VALUE_HEADS * HEAD_SIZE),
            "seq",
            scatter_dimension=0,
            tiled=True,
        ),
    )
    key_back = (
        key_pullback(local_key_rows.reshape(local_rows, KEY_VALUE_HEADS, HEAD_SIZE))[0]
        .reshape(local_rows, KEY_VALUE_HEADS * HEAD_SIZE)
        .astype(jnp.bfloat16)
    )
    query_rot_grad = jnp.transpose(grad_query_sum, (2, 0, 1, 3)).reshape(
        local_rows, QUERY_HEAD_COUNT, HEAD_SIZE
    )
    query_back = (
        pull_query(query_rot_grad)[0]
        .reshape(local_rows, QUERY_HEAD_COUNT * HEAD_SIZE)
        .astype(jnp.bfloat16)
    )
    value_back = value_own.astype(jnp.bfloat16)
    grad_query = jnp.einsum(
        "nd,nk->dk", first_activation, query_back, preferred_element_type=jnp.float32
    )
    grad_key = jnp.einsum(
        "nd,nk->dk", first_activation, key_back, preferred_element_type=jnp.float32
    )
    grad_value = jnp.einsum(
        "nd,nk->dk", first_activation, value_back, preferred_element_type=jnp.float32
    )
    grad_act_one = jnp.einsum(
        "nk,dk->nd", query_back, full_query, preferred_element_type=jnp.float32
    )
    grad_act_one = grad_act_one + jnp.einsum(
        "nk,dk->nd", key_back, complete_key, preferred_element_type=jnp.float32
    )
    grad_act_one = grad_act_one + jnp.einsum(
        "nk,dk->nd", value_back, complete_value, preferred_element_type=jnp.float32
    )
    input_norm_grad, grad_gain_one = pull_norm_one(grad_act_one)
    input_grad = (grad_residual + input_norm_grad)[None]
    shard_grads = (
        lax.psum_scatter(grad_query, "seq", scatter_dimension=0, tiled=True),
        lax.psum_scatter(grad_key, "seq", scatter_dimension=0, tiled=True),
        lax.psum_scatter(grad_value, "seq", scatter_dimension=0, tiled=True),
        lax.psum_scatter(grad_out, "seq", scatter_dimension=0, tiled=True),
        lax.psum_scatter(grad_gate, "seq", scatter_dimension=0, tiled=True),
        lax.psum_scatter(grad_up, "seq", scatter_dimension=0, tiled=True),
        lax.psum_scatter(grad_down, "seq", scatter_dimension=0, tiled=True),
        lax.psum_scatter(grad_gain_one, "seq", scatter_dimension=0, tiled=True),
        lax.psum_scatter(grad_gain_two, "seq", scatter_dimension=0, tiled=True),
    )
    gradients = lax.psum(
        (
            shard_grads[0],
            shard_grads[1],
            shard_grads[2],
            shard_grads[3],
            shard_grads[4],
            shard_grads[5],
            shard_grads[6],
            shard_grads[7],
            shard_grads[8],
        ),
        "dp",
    )
    squares = jnp.float32(0.0)
    for gradient in gradients:
        squares = squares + jnp.sum(gradient * gradient)
    gradient_norm = jnp.sqrt(lax.psum(squares, "seq"))
    clip_factor = jnp.minimum(1.0, jnp.sqrt(jnp.float32(PARAMS)) / (gradient_norm + 1e-06))
    momenta = [
        momentum_beta * moment + clip_factor * gradient
        for moment, gradient in zip(moments, gradients)
    ]
    updated = [
        master * (1.0 - learning_rate * weight_decay) - learning_rate * momentum
        for master, momentum in zip(masters, momenta)
    ]
    return (
        output,
        input_grad,
        momenta[0],
        momenta[1],
        momenta[2],
        momenta[3],
        momenta[4],
        momenta[5],
        momenta[6],
        momenta[7],
        momenta[8],
        updated[0],
        updated[1],
        updated[2],
        updated[3],
        updated[4],
        updated[5],
        updated[6],
        updated[7],
        updated[8],
        gradient_norm,
    )


def solution(mesh):
    return jax.shard_map(
        per_device,
        mesh=mesh,
        in_specs=(
            P("dp", "seq", None),
            P("dp", "seq", None),
            P("dp", None),
            P("seq", None),
            P("seq", None),
            P("seq", None),
            P("seq", None),
            P("seq", None),
            P("seq", None),
            P("seq", None),
            P("seq"),
            P("seq"),
            P("seq", None),
            P("seq", None),
            P("seq", None),
            P("seq", None),
            P("seq", None),
            P("seq", None),
            P("seq", None),
            P("seq"),
            P("seq"),
        ),
        out_specs=(
            P("dp", "seq", None),
            P("dp", "seq", None),
            P("seq", None),
            P("seq", None),
            P("seq", None),
            P("seq", None),
            P("seq", None),
            P("seq", None),
            P("seq", None),
            P("seq"),
            P("seq"),
            P("seq", None),
            P("seq", None),
            P("seq", None),
            P("seq", None),
            P("seq", None),
            P("seq", None),
            P("seq", None),
            P("seq"),
            P("seq"),
            P(),
        ),
        check_vma=False,
    )
```

profile of v0, /device:TPU:0, one launch (start us, length us, event | category | flops | bytes accessed | tf_op | source)
XLA Modules:
  0.0 1444.6 jit_solution(14525401871639429542)
XLA Ops:
  7.2 2.3 convert_element_type.172
  10.6 3.5 convert_element_type.183
  14.2 3.5 convert_element_type.184
  17.7 3.4 convert_element_type.186
  23.6 11.7 all-reduce.11
  35.5 19.6 %all_gather.34 = bf16[1152,384]{1,0:T(8,128)(2,1)S(1)} all-gather(bf16[288,384]{1,0:T(8,128)(2,1)S(1)} %convert_element_type.169), channel_id=1, replica_groups=mesh['seq'=4,'dp'=8] {'seq'}, dimensions={0}, use_global_device_ids=true | all-gather | bytes 1105920 | tf_op jit(solution)/shard_map/all_gather | solution.py:112
  55.1 1.5 copy.71
  56.8 11.8 all_gather.37
  69.2 15.4 %all_gather.38 = bf16[1024,384]{1,0:T(8,128)(2,1)S(1)} all-gather(bf16[256,384]{1,0:T(8,128)(2,1)S(1)} %convolution_convert_fusion.1), channel_id=1, replica_groups=mesh['seq'=4,'dp'=8] {'seq'}, dimensions={0}, use_global_device_ids=true | all-gather | bytes 983040 | tf_op jit(solution)/shard_map/all_gather | solution.py:154
  88.7 23.0 %all_gather.35 = bf16[1024,384]{0,1:T(8,128)(2,1)S(1)} all-gather(bf16[256,384]{0,1:T(8,128)(2,1)S(1)} %bitcast.215), channel_id=1, replica_groups=mesh['seq'=4,'dp'=8] {'seq'}, dimensions={0}, use_global_device_ids=true | all-gather | bytes 983040 | tf_op jit(solution)/shard_map/all_gather | solution.py:153
  111.7 5.2 copy.72
  117.0 2.8 fusion.82
  121.1 10.1 while.36
  123.7 4.4 conditional.6
  124.1 2.1 fusion.8
  126.3 1.8 fusion.15
  132.1 3.1 multiply_reduce_fusion.8
  137.2 54.5 %all-gather.10.cloned.1.call-done = bf16[1152,3072]{1,0:T(8,128)(2,1)} async-done(((bf16[288,3072]{1,0:T(8,128)(2,1)}), bf16[1152,3072]{1,0:T(8,128)(2,1)}) %all-gather.10.cloned.1.call-update) | async-done | bytes 7077904 | tf_op jit(solution)/shard_map/all_gather | solution.py:115
  191.7 7.1 fusion.110
  198.8 71.9 %all-gather.12.cloned.1.call-done = bf16[1152,3072]{1,0:T(8,128)(2,1)} async-done(((bf16[288,3072]{1,0:T(8,128)(2,1)}), bf16[1152,3072]{1,0:T(8,128)(2,1)}) %all-gather.12.cloned.1.call-update) | async-done | bytes 7077904 | tf_op jit(solution)/shard_map/all_gather | solution.py:116
  270.7 7.1 fusion.111
  277.8 71.9 %all-gather.14.cloned.1.call-done = bf16[3072,1152]{1,0:T(8,128)(2,1)} async-done(((bf16[768,1152]{1,0:T(8,128)(2,1)}), bf16[3072,1152]{1,0:T(8,128)(2,1)}) %all-gather.14.cloned.1.call-update) | async-done | bytes 7077904 | tf_op jit(solution)/shard_map/all_gather | solution.py:117
  349.7 9.1 multiply_convert_fusion
  358.8 6.4 fusion.112
  365.3 2.6 multiply_reduce_fusion.5
  370.2 2.2 fusion.60
  372.4 2.7 copy.74
  375.1 2.3 multiply_reduce_fusion.6
  380.2 16.2 %while.37 = (s32[]{:T(128)}, f32[6,3,256,64]{2,3,1,0:T(8,128)S(1)}, f32[1024,6,64]{0,2,1:T(8,128)}, f32[1024,6,64]{0,2,1:T(8,128)}, s32[]{:T(128)}, /*index=5*/s...) while((s32[]{:T(128)}, f32[6,3,256,64]{2,3,1,0:T(8,128)S(1)}, ...), condition=%wide.region_14.15_spmd.clone, body=%wide.region_11.14_spmd.clone.sunk | while | flops 1530135040 | bytes 83410128 | solution.py:294
  382.8 11.1 conditional.7
  384.7 2.7 fusion.27
  387.5 1.5 fusion.43
  391.0 1.7 fusion.38
  397.3 41.3 %reduce-scatter.10.cloned.1.call-done = f32[256,384]{0,1:T(8,128)} async-done(((f32[1024,384]{0,1:T(8,128)}), f32[256,384]{0,1:T(8,128)}) %reduce-scatter.10.cloned.1.call-update) | async-done | bytes 393232 | tf_op jit(solution)/shard_map/reduce_scatter | solution.py:298
  439.7 1.8 fusion.86
  441.6 31.5 %reduce-scatter.12.cloned.1.call-done = f32[256,384]{0,1:T(8,128)} async-done(((f32[1024,384]{0,1:T(8,128)}), f32[256,384]{0,1:T(8,128)}) %reduce-scatter.12.cloned.1.call-update) | async-done | bytes 393232 | tf_op jit(solution)/shard_map/reduce_scatter | solution.py:304
  473.1 2.8 fusion.94
  477.2 4.4 fusion.91
  481.9 3.4 fusion.88
  486.4 8.5 fusion.114
  495.2 8.5 fusion.115
  504.8 8.7 fusion.78
  513.6 31.8 %reduce-scatter.18.cloned.1.call-done = f32[288,384]{1,0:T(8,128)} async-done(((f32[1152,384]{1,0:T(8,128)}), f32[288,384]{1,0:T(8,128)}) %reduce-scatter.18.cloned.1.call-update) | async-done | bytes 442384 | tf_op jit(solution)/shard_map/reduce_scatter | solution.py:348
  545.4 64.9 %reduce-scatter.20.cloned.1.call-done = f32[288,1152]{1,0:T(8,128)} async-done(((f32[1152,1152]{1,0:T(8,128)}), f32[288,1152]{1,0:T(8,128)}) %reduce-scatter.20.cloned.1.call-update) | async-done | bytes 1327120 | tf_op jit(solution)/shard_map/reduce_scatter | solution.py:349
  610.2 65.0 %reduce-scatter.14.cloned.1.call-done = f32[288,1152]{1,0:T(8,128)} async-done(((f32[1152,1152]{1,0:T(8,128)}), f32[288,1152]{1,0:T(8,128)}) %reduce-scatter.14.cloned.1.call-update) | async-done | bytes 1327120 | tf_op jit(solution)/shard_map/reduce_scatter | solution.py:346
  675.2 136.7 %reduce-scatter.22.cloned.1.call-done = f32[288,3072]{1,0:T(8,128)} async-done(((f32[1152,3072]{1,0:T(8,128)}), f32[288,3072]{1,0:T(8,128)}) %reduce-scatter.22.cloned.1.call-update) | async-done | bytes 3538960 | tf_op jit(solution)/shard_map/reduce_scatter | solution.py:350
  811.9 136.8 %reduce-scatter.24.cloned.1.call-done = f32[288,3072]{1,0:T(8,128)} async-done(((f32[1152,3072]{1,0:T(8,128)}), f32[288,3072]{1,0:T(8,128)}) %reduce-scatter.24.cloned.1.call-update) | async-done | bytes 3538960 | tf_op jit(solution)/shard_map/reduce_scatter | solution.py:351
  948.7 136.6 %reduce-scatter.26.cloned.1.call-done = f32[768,1152]{1,0:T(8,128)} async-done(((f32[3072,1152]{1,0:T(8,128)}), f32[768,1152]{1,0:T(8,128)}) %reduce-scatter.26.cloned.1.call-update) | async-done | bytes 3538960 | tf_op jit(solution)/shard_map/reduce_scatter | solution.py:352
  1086.0 2.9 fusion.113
  1089.0 6.2 fusion.62
  1097.2 15.2 %all-reduce.10 = (f32[1152]{0:T(1024)S(1)}, f32[1152]{0:T(1024)S(1)}) all-reduce(f32[1152]{0:T(1024)S(1)} %get-tuple-element.816, f32[1152]{0:T(1024)S(1)} %get-tuple-element.814), channel_id=11, replica_groups=mesh['seq'=4,'dp'=8] {'seq'}, use_global_device_ids=true, to_apply=%region_40.41.clone | all-reduce | flops 2304 | bytes 18432
  1112.6 14.6 %all-reduce.8 = (f32[288]{0:T(512)S(1)}, f32[288]{0:T(512)S(1)}) all-reduce(f32[288]{0:T(512)S(1)} %dynamic-slice.3, f32[288]{0:T(512)S(1)} %dynamic-slice.5), channel_id=1, replica_groups=mesh['seq'=4,'dp'=8] {'dp'}, use_global_device_ids=true, to_apply=%region_41.42 | all-reduce | flops 576 | bytes 4608 | tf_op jit(solution)/shard_map/psum | solution.py:356
  1128.5 246.4 %all-reduce.14.cloned.1.call-done = (f32[288,1152]{1,0:T(8,128)}, f32[288,384]{1,0:T(8,128)}, f32[288,384]{1,0:T(8,128)}, f32[288,1152]{1,0:T(8,128)}, f32[288,3...) async-done(((f32[288,1152]{1,0:T(8,128)}, f32[288,384]{1,0:T(8,128)}, f32[288,384]{1,0:T(8,128)}, f32[288,1152]{1,0:T(8,128)}, f32[288,3072]{1,0:T(8,128)}, ...) | async-done | bytes 14155792 | tf_op jit(solution)/shard_map/psum | solution.py:356
  1374.9 1.9 multiply_reduce_fusion.10
  1376.8 2.3 multiply_reduce_fusion.4
  1379.1 1.7 multiply_reduce_fusion.9
  1380.8 2.3 multiply_reduce_fusion.3
  1383.1 1.5 multiply_reduce_fusion.2
  1395.8 10.6 psum.79
  1408.3 8.5 multiply_subtract_fusion
  1418.0 4.6 multiply_subtract_fusion.1
  1423.3 6.3 multiply_subtract_fusion.2
  1429.7 1.8 multiply_subtract_fusion.3
  1434.7 1.8 multiply_subtract_fusion.4
  (259 shorter events, 45.2 us)
Async XLA Ops:
  7.2 2.5 copy-start.22
  7.2 104.5 %all-gather.6.cloned.1.call-start = ((), (), s32[]{:S(2)}) async-start(), calls=%async_computation.9 | async-start | bytes 3317760 | tf_op jit(solution)/shard_map/all_gather | solution.py:111
  9.6 122.5 %all-gather.8.cloned.1.call-start = ((), (), s32[]{:S(2)}) async-start(), calls=%async_computation.10 | async-start | bytes 3317760 | tf_op jit(solution)/shard_map/all_gather | solution.py:114
  10.6 181.1 %all-gather.10.cloned.1.call-start = ((), (), s32[]{:S(2)}) async-start(), calls=%async_computation.11 | async-start | bytes 8847360 | tf_op jit(solution)/shard_map/all_gather | solution.py:115
  14.1 256.6 %all-gather.12.cloned.1.call-start = ((), (), s32[]{:S(2)}) async-start(), calls=%async_computation.12 | async-start | bytes 8847360 | tf_op jit(solution)/shard_map/all_gather | solution.py:116
  17.7 332.0 %all-gather.14.cloned.1.call-start = ((), (), s32[]{:S(2)}) async-start(), calls=%async_computation.13 | async-start | bytes 8847360 | tf_op jit(solution)/shard_map/all_gather | solution.py:117
  21.2 14.3 copy-start.36
  21.2 417.4 %reduce-scatter.10.cloned.1.call-start = ((), (), s32[]{:S(2)}) async-start(), calls=%async_computation.14 | async-start | bytes 1966080 | tf_op jit(solution)/shard_map/reduce_scatter | solution.py:298
  35.4 81.6 %copy-start.54 = (f32[1152]{0:T(1024)}, f32[1152]{0:T(1024)S(1)}, u32[]{:S(2)}) copy-start(f32[1152]{0:T(1024)S(1)} %convert_element_type.166) | copy-start | bytes 13828
  35.5 21.1 %copy-start.34 = (f32[288,384]{1,0:T(8,128)S(1)}, f32[288,384]{1,0:T(8,128)}, u32[]{:S(2)}) copy-start(f32[288,384]{1,0:T(8,128)} %param.34) | copy-start | bytes 1327108
  35.5 21.1 %copy-start = (bf16[1,256,1152]{2,1,0:T(8,128)(2,1)S(1)}, bf16[1,256,1152]{2,1,0:T(8,128)(2,1)}, u32[]{:S(2)}) copy-start(bf16[1,256,1152]{2,1,0:T(8,128)(2,1)} %param.29) | copy-start | bytes 1769476
  55.1 13.5 copy-start.13
  56.8 11.8 copy-start.58
  68.6 16.0 %copy-start.29 = (bf16[1152,384]{1,0:T(8,128)(2,1)}, bf16[1152,384]{1,0:T(8,128)(2,1)S(1)}, u32[]{:S(2)}) copy-start(bf16[1152,384]{1,0:T(8,128)(2,1)S(1)} %all_gather.37) | copy-start | bytes 2654212
  68.6 48.3 %copy-start.56 = (f32[256]{0:T(256)}, f32[256]{0:T(256)S(1)}, u32[]{:S(2)}) copy-start(f32[256]{0:T(256)S(1)} %fusion.101) | copy-start | bytes 3076
  69.2 17.2 %copy-start.67 = (s32[1,2]{1,0:T(1,128)S(1)}, s32[1,2]{1,0:T(1,128)}, u32[]{:S(2)}) copy-start(s32[1,2]{1,0:T(1,128)} %param.31) | copy-start | bytes 28
  69.2 18.9 %copy-start.46 = (bf16[384,1152]{1,0:T(8,128)(2,1)S(1)}, bf16[384,1152]{1,0:T(8,128)(2,1)}, u32[]{:S(2)}) copy-start(bf16[384,1152]{1,0:T(8,128)(2,1)} %copy.71) | copy-start | bytes 2654212
  88.1 31.7 %copy-start.47 = (f32[256,32]{0,1:T(8,128)}, f32[256,32]{0,1:T(8,128)S(1)}, u32[]{:S(2)}) copy-start(f32[256,32]{0,1:T(8,128)S(1)} %get-tuple-element.922) | copy-start | bytes 98308
  88.1 31.7 %copy-start.49 = (f32[256,32]{0,1:T(8,128)}, f32[256,32]{0,1:T(8,128)S(1)}, u32[]{:S(2)}) copy-start(f32[256,32]{0,1:T(8,128)S(1)} %get-tuple-element.923) | copy-start | bytes 98308
  124.1 2.2 copy-start.11
  358.8 6.4 copy-start.43
  358.8 6.4 copy-start.42
  358.8 6.5 copy-start.26
  358.8 6.5 copy-start.68
  365.3 2.7 copy-start.32
  368.0 2.2 copy-start.31
  384.7 2.7 copy-start.1
  384.7 2.7 copy-start.16
  389.0 2.0 copy-start.18
  396.5 42.1 %copy-start.48 = (f32[256,32]{0,1:T(8,128)S(1)}, f32[256,32]{0,1:T(8,128)}, u32[]{:S(2)}) copy-start(f32[256,32]{0,1:T(8,128)} %copy-done.47) | copy-start | bytes 98308
  396.5 42.1 %copy-start.50 = (f32[256,32]{0,1:T(8,128)S(1)}, f32[256,32]{0,1:T(8,128)}, u32[]{:S(2)}) copy-start(f32[256,32]{0,1:T(8,128)} %copy-done.49) | copy-start | bytes 98308
  396.5 43.2 %copy-start.55 = (f32[1152]{0:T(1024)S(1)}, f32[1152]{0:T(1024)}, u32[]{:S(2)}) copy-start(f32[1152]{0:T(1024)} %copy-done.54) | copy-start | bytes 13828
  396.5 43.2 %copy-start.57 = (f32[256]{0:T(256)S(1)}, f32[256]{0:T(256)}, u32[]{:S(2)}) copy-start(f32[256]{0:T(256)} %copy-done.56) | copy-start | bytes 3076
  396.5 76.6 %reduce-scatter.12.cloned.1.call-start = ((), (), s32[]{:S(2)}) async-start(), calls=%async_computation.15 | async-start | bytes 1966080 | tf_op jit(solution)/shard_map/reduce_scatter | solution.py:304
  397.3 116.3 %reduce-scatter.16.cloned.1.call-start = ((), (), s32[]{:S(2)}) async-start(), calls=%async_computation.17 | async-start | bytes 2211840 | tf_op jit(solution)/shard_map/reduce_scatter | solution.py:347
  441.6 103.8 %reduce-scatter.18.cloned.1.call-start = ((), (), s32[]{:S(2)}) async-start(), calls=%async_computation.18 | async-start | bytes 2211840 | tf_op jit(solution)/shard_map/reduce_scatter | solution.py:348
  476.0 134.3 %reduce-scatter.20.cloned.1.call-start = ((), (), s32[]{:S(2)}) async-start(), calls=%async_computation.19 | async-start | bytes 6635520 | tf_op jit(solution)/shard_map/reduce_scatter | solution.py:349
  481.6 193.6 %reduce-scatter.14.cloned.1.call-start = ((), (), s32[]{:S(2)}) async-start(), calls=%async_computation.16 | async-start | bytes 6635520 | tf_op jit(solution)/shard_map/reduce_scatter | solution.py:346
  485.4 326.6 %reduce-scatter.22.cloned.1.call-start = ((), (), s32[]{:S(2)}) async-start(), calls=%async_computation.20 | async-start | bytes 17694720 | tf_op jit(solution)/shard_map/reduce_scatter | solution.py:350
  494.9 453.8 %reduce-scatter.24.cloned.1.call-start = ((), (), s32[]{:S(2)}) async-start(), calls=%async_computation.21 | async-start | bytes 17694720 | tf_op jit(solution)/shard_map/reduce_scatter | solution.py:351
  503.7 581.6 %reduce-scatter.26.cloned.1.call-start = ((), (), s32[]{:S(2)}) async-start(), calls=%async_computation.22 | async-start | bytes 17694720 | tf_op jit(solution)/shard_map/reduce_scatter | solution.py:352
  513.5 861.4 %all-reduce.14.cloned.1.call-start = ((), (), s32[]{:S(2)}) async-start(), calls=%async_computation.23 | async-start | bytes 28311552 | tf_op jit(solution)/shard_map/psum | solution.py:356
  1086.0 3.0 copy-start.27
  1086.0 3.0 copy-start.41
  1089.0 6.2 copy-start.14
  1096.5 32.0 %copy-start.59 = (f32[256]{0:T(256)S(1)}, f32[256]{0:T(256)}, u32[]{:S(2)}) copy-start(f32[256]{0:T(256)} %copy-done.58) | copy-start | bytes 3076
  1374.9 8.1 copy-start.6
  1383.1 2.0 copy-start.8
  1385.1 2.0 copy-start.10
  1394.4 12.7 copy-start.61
  1394.4 12.7 copy-start.65
  1394.4 13.3 copy-start.63
  1394.4 13.3 copy-start.66
  1408.3 8.5 copy-start.4
  1408.3 8.5 copy-start.9
  1408.3 9.7 copy-start.28
  1418.0 4.6 copy-start.5
  1418.0 5.3 copy-start.7
  1423.3 6.3 copy-start.21
  1423.3 6.3 copy-start.23
  1423.3 6.3 copy-start.44
  1429.6 2.9 copy-start.53
  1429.6 4.4 copy-start.45
  1431.5 2.5 copy-start.24
  (20 other events, 25.1 us)
Sparse Core Ops, SparseCore 0:
  10.4 49.8 all-gather.5
  62.7 47.9 all-gather.7
  113.1 78.5 all-gather.9
  194.0 76.6 all-gather.11
  273.0 76.6 all-gather.13
  396.6 41.9 reduce-scatter.9
  442.2 30.9 reduce-scatter.11
  476.7 32.4 reduce-scatter.15
  512.9 32.4 reduce-scatter.17
  548.2 61.9 reduce-scatter.19
  613.2 61.9 reduce-scatter.13
  678.3 133.6 reduce-scatter.21
  815.1 133.6 reduce-scatter.23
  951.7 133.5 reduce-scatter.25
  1088.1 286.7 all-reduce.13
where the time goes:
time: 1450 us; the launch traced here: 1440 us
  waiting for transfers between devices  1090 us (75%)
  blocking collectives  122 us (8%)
  matrix products  102 us (7%)
  other arithmetic  63.3 us (4%)
  local copies, waits for them, and re-layouts  32.4 us (2%)
  between operations  24.8 us (2%)
    psum x1, waiting for transfers between devices, per_device(): lax.psum((shard_grads[0], shard_grads[1], shard_grads[2], shard_grads[3],...  246 us
    reduce_scatter x1, waiting for transfers between devices, per_device(): lax.psum_scatter(grad_up, 'seq', scatter_dimension=0, tiled=True)  137 us
    reduce_scatter x1, waiting for transfers between devices, per_device(): lax.psum_scatter(grad_gate, 'seq', scatter_dimension=0, tiled=True)  137 us
    reduce_scatter x1, waiting for transfers between devices, per_device(): lax.psum_scatter(grad_down, 'seq', scatter_dimension=0, tiled=True)  137 us
    all_gather x1, waiting for transfers between devices, per_device(): lax.all_gather(shard_up, 'seq', axis=0, tiled=True)  71.9 us
    all_gather x1, waiting for transfers between devices, per_device(): lax.all_gather(shard_down, 'seq', axis=0, tiled=True)  71.9 us
    reduce_scatter x1, waiting for transfers between devices, per_device(): lax.psum_scatter(grad_query, 'seq', scatter_dimension=0, tiled=True)  65 us
    reduce_scatter x1, waiting for transfers between devices, per_device(): lax.psum_scatter(grad_out, 'seq', scatter_dimension=0, tiled=True)  64.9 us
  transfers between devices with their start and end apart: 15, of which 12 were waited for; matrix products, arithmetic and copies ran while one was open for 7% of the time, Pallas kernels for 0%

commit v1 on v0

--- a/solution.py
+++ b/solution.py
@@ -405,9 +405,407 @@
     )
 
 
+BF = jnp.bfloat16
+F32 = jnp.float32
+
+
+def swap_x(value):
+    return lax.ppermute(value, "seq", [(i, i ^ 1) for i in range(4)])
+
+
+def swap_y(value):
+    return lax.ppermute(value, "seq", [(i, i ^ 2) for i in range(4)])
+
+
+def swap_diagonal(value):
+    return lax.ppermute(value, "seq", [(i, i ^ 3) for i in range(4)])
+
+
+def swap_core(value):
+    return lax.ppermute(value, "dp", [(i, i ^ 1) for i in range(8)])
+
+
+def move_up(value):
+    return lax.ppermute(value, "dp", [(i, i + 2) for i in range(6)])
+
+
+def move_down(value):
+    return lax.ppermute(value, "dp", [(i + 2, i) for i in range(6)])
+
+
+def dot(left, right):
+    return jnp.dot(left, right, preferred_element_type=F32)
+
+
+def dot_rows(left, right):
+    return lax.dot_general(left, right, (((0,), (0,)), ((), ())), preferred_element_type=F32)
+
+
+def dot_transposed(left, right):
+    return lax.dot_general(left, right, (((1,), (1,)), ((), ())), preferred_element_type=F32)
+
+
+def gather_plane(first, second):
+    x_first = swap_x(first)
+    y_first = swap_y(first)
+    x_second = swap_x(second)
+    y_second = swap_y(second)
+    d_first = swap_x(y_first)
+    d_second = swap_y(x_second)
+    return (x_first, x_second), (y_first, y_second), (d_first, d_second)
+
+
+def scatter_plane(own, for_x, for_y, for_d):
+    y_relay = swap_x(for_d[0].astype(BF))
+    x_relay = swap_y(for_d[1].astype(BF))
+    x_first = swap_x(for_x[0].astype(BF))
+    y_second = swap_y(for_y[1].astype(BF))
+    x_second = swap_x((for_x[1] + x_relay).astype(BF))
+    y_first = swap_y((for_y[0] + y_relay).astype(BF))
+    return own[0] + x_first + y_first, own[1] + x_second + y_second
+
+
+def halves(value):
+    middle = value.shape[0] // 2
+    return value[:middle], value[middle:]
+
+
+def scatter_line(chunks, place):
+    def pick(number):
+        return lax.dynamic_index_in_dim(chunks, jnp.clip(number, 0, 3), 0, keepdims=False)
+
+    upward = downward = None
+    for step in (1, 2, 3):
+        up_part = pick(place + 4 - step).astype(F32)
+        down_part = pick(place - 4 + step).astype(F32)
+        if upward is not None:
+            up_part = up_part + upward
+            down_part = down_part + downward
+        upward = move_up(up_part.astype(BF))
+        downward = move_down(down_part.astype(BF))
+    return pick(place).astype(F32) + upward + downward
+
+
+def gather_line(own):
+    below, above = [own], [own]
+    for _ in range(3):
+        below.append(move_up(below[-1]))
+        above.append(move_down(above[-1]))
+    return [own] + [above[j] + below[4 - j] for j in (1, 2, 3)]
+
+
+def sum_everywhere(value):
+    value = value + swap_core(value)
+    value = value + swap_x(value)
+    value = value + swap_y(value)
+    value = value + lax.ppermute(value, "dp", [(i, i ^ 2) for i in range(8)])
+    return value + lax.ppermute(value, "dp", [(i, i ^ 4) for i in range(8)])
+
+
+def natural(blocks, own_place):
+    result = jnp.stack(blocks)
+    order = jnp.arange(4, dtype=jnp.int32) ^ own_place
+    return result[order]
+
+
+def put_rows(target, block, row):
+    return lax.dynamic_update_slice(target, block, (row, jnp.int32(0)))
+
+
+def fast_device(
+    tokens,
+    cotangent,
+    picture_starts,
+    query_weight,
+    key_matrix,
+    value_matrix,
+    out_weight,
+    gate_weight,
+    up_weight,
+    down_weight,
+    attention_gain,
+    feed_gain,
+    query_moment,
+    key_velocity,
+    value_velocity,
+    out_moment,
+    gate_moment,
+    up_moment,
+    down_moment,
+    attention_moment,
+    feed_moment,
+):
+    masters = (
+        query_weight,
+        key_matrix,
+        value_matrix,
+        out_weight,
+        gate_weight,
+        up_weight,
+        down_weight,
+        attention_gain,
+        feed_gain,
+    )
+    moments = (
+        query_moment,
+        key_velocity,
+        value_velocity,
+        out_moment,
+        gate_moment,
+        up_moment,
+        down_moment,
+        attention_moment,
+        feed_moment,
+    )
+    me = lax.axis_index("seq")
+    line = lax.axis_index("dp") // 2
+    core = lax.axis_index("dp") % 2
+    rows = tokens.shape[1]
+    width = tokens.shape[2]
+    shard = query_weight.shape[0]
+    half = shard // 2
+    hidden_own = down_weight.shape[0]
+    kv_width = KEY_VALUE_HEADS * HEAD_SIZE
+    group = QUERY_HEAD_COUNT // KEY_VALUE_HEADS
+    places = [me, me ^ 1, me ^ 2, me ^ 3]
+
+    gains = jnp.stack([attention_gain, feed_gain]).astype(BF)
+    gains_x = swap_x(gains)
+    gains_y = swap_y(gains)
+    gains_d = swap_x(gains_y)
+    all_gains = natural([gains, gains_x, gains_y, gains_d], me)
+    gain_one = all_gains[:, 0].reshape(width).astype(F32)
+    gain_two = all_gains[:, 1].reshape(width).astype(F32)
+
+    def fetch_rows(shard_value):
+        mine = lax.dynamic_slice_in_dim(shard_value, core * half, half, 0)
+        pieces = gather_plane(*halves(mine))
+        fetched = jnp.stack([jnp.concatenate(pair) for pair in pieces])
+        other = swap_core(fetched)
+        full = jnp.zeros((4 * shard, shard_value.shape[1]), BF)
+        full = put_rows(full, shard_value, me * shard)
+        for j in range(3):
+            start = places[j + 1] * shard
+            full = put_rows(full, fetched[j], start + core * half)
+            full = put_rows(full, other[j], start + (1 - core) * half)
+        return full
+
+    shard_qkv = jnp.concatenate([query_weight, key_matrix, value_matrix], axis=1).astype(BF)
+    full_qkv = fetch_rows(shard_qkv)
+    full_out = fetch_rows(out_weight.astype(BF))
+
+    shard_gate = gate_weight.astype(BF)
+    shard_up = up_weight.astype(BF)
+
+    def columns_for(place, first, count):
+        at = (first, place * hidden_own)
+        size = (count, hidden_own)
+        return jnp.concatenate(
+            [lax.dynamic_slice(shard_gate, at, size), lax.dynamic_slice(shard_up, at, size)], axis=1
+        )
+
+    sent = [columns_for(place, core * half, half) for place in places[1:]]
+    fetched = [swap_x(sent[0]), swap_y(sent[1]), swap_diagonal(sent[2])]
+    other = [swap_core(block) for block in fetched]
+    full_gu = jnp.zeros((width, 2 * hidden_own), BF)
+    full_gu = put_rows(full_gu, columns_for(me, jnp.int32(0), shard), me * shard)
+    for j in range(3):
+        start = places[j + 1] * shard
+        full_gu = put_rows(full_gu, fetched[j], start + core * half)
+        full_gu = put_rows(full_gu, other[j], start + (1 - core) * half)
+    own_down = down_weight.astype(BF)
+
+    token_positions = me * rows + jnp.arange(rows, dtype=jnp.int32)
+    starts = picture_starts[0]
+    query_piece = piece_number(token_positions, starts)
+    key_positions = jnp.concatenate(
+        [place * rows + jnp.arange(rows, dtype=jnp.int32) for place in places]
+    )
+    key_pieces = piece_number(key_positions, starts)
+    allowed = visible(token_positions, query_piece, key_positions, key_pieces)
+
+    upstream_low = cotangent[0]
+    pieces = gather_plane(*halves(upstream_low))
+    every_upstream = jnp.concatenate([upstream_low] + [part for pair in pieces for part in pair])
+
+    layer_input = tokens[0].astype(F32)
+    normed_one, pull_norm_one = jax.vjp(rms_scale, layer_input, gain_one)
+    first_activation = normed_one.astype(BF)
+    linear = dot(first_activation, full_qkv)
+    rotation = partial(apply_rotary, token_positions=token_positions)
+    heads_qk = QUERY_HEAD_COUNT + KEY_VALUE_HEADS
+    rotated, pull_rotation = jax.vjp(
+        rotation, linear[:, : width + kv_width].reshape(rows, heads_qk, HEAD_SIZE)
+    )
+    rotated = rotated.astype(BF)
+    query = jnp.transpose(
+        rotated[:, :QUERY_HEAD_COUNT].reshape(rows, KEY_VALUE_HEADS, group, HEAD_SIZE), (1, 2, 0, 3)
+    ).reshape(KEY_VALUE_HEADS, group * rows, HEAD_SIZE)
+    key_value = jnp.concatenate(
+        [rotated[:, QUERY_HEAD_COUNT:].reshape(rows, kv_width), linear[:, width + kv_width :].astype(BF)],
+        axis=1,
+    )
+    pieces = gather_plane(*halves(key_value))
+    every_kv = jnp.concatenate([key_value] + [part for pair in pieces for part in pair])
+    every_kv = jnp.transpose(
+        every_kv.reshape(4 * rows, 2, KEY_VALUE_HEADS, HEAD_SIZE), (1, 2, 0, 3)
+    )
+    keys, values = every_kv[0], every_kv[1]
+    mask = jnp.broadcast_to(allowed[None], (group, rows, 4 * rows)).reshape(group * rows, 4 * rows)
+    scores = jnp.einsum("hqd,hkd->hqk", query, keys, preferred_element_type=F32)
+    exponent = jnp.where(mask[None], jnp.exp(scores * 0.125), 0.0)
+    totals = jnp.sum(exponent, axis=-1, keepdims=True)
+    exponent_low = exponent.astype(BF)
+    attended = (
+        jnp.einsum("hqk,hkd->hqd", exponent_low, values, preferred_element_type=F32) / totals
+    )
+
+    def by_rows(value):
+        value = value.reshape(KEY_VALUE_HEADS, group, rows, HEAD_SIZE)
+        return jnp.transpose(value, (2, 0, 1, 3)).reshape(rows, width)
+
+    attention = by_rows(attended).astype(BF)
+    residual = layer_input + dot(attention, full_out)
+    normed_two, pull_norm_two = jax.vjp(rms_scale, residual, gain_two)
+    act_two = normed_two.astype(BF)
+
+    pieces = gather_plane(*halves(act_two))
+    every_act = jnp.concatenate([act_two] + [part for pair in pieces for part in pair])
+    both = dot(every_act, full_gu)
+    hidden_full, pull_swiglu = jax.vjp(swiglu, both[:, :hidden_own], both[:, hidden_own:])
+    hidden = hidden_full.astype(BF)
+    grad_hidden = dot_transposed(every_upstream, own_down)
+    grad_gate_full, grad_up_full = pull_swiglu(grad_hidden)
+    both_back = jnp.concatenate([grad_gate_full, grad_up_full], axis=1).astype(BF)
+    grad_act = dot_transposed(both_back, full_gu)
+
+    def token_blocks(value):
+        return [halves(value[j * rows : (j + 1) * rows]) for j in range(4)]
+
+    grad_act_two = jnp.concatenate(scatter_plane(*token_blocks(grad_act)))
+    layer_part = dot(hidden, own_down)
+    output = (residual + jnp.concatenate(scatter_plane(*token_blocks(layer_part)))).astype(BF)[None]
+    grad_gu = dot_rows(every_act, both_back)
+    grad_down = dot_rows(hidden, every_upstream)
+
+    gu_parts = grad_gu.reshape(4, 2, half, 4, 2 * hidden_own // 4)
+    gu_keep = lax.dynamic_index_in_dim(gu_parts, core, 1, keepdims=False)
+    gu_send = lax.dynamic_index_in_dim(gu_parts, 1 - core, 1, keepdims=False)
+    gu_pair = gu_keep + swap_core(gu_send.astype(BF))
+    gu_own = scatter_line(jnp.transpose(gu_pair, (2, 0, 1, 3)), line).astype(BF)
+    down_parts = grad_down.reshape(2, 4, hidden_own // 8, width)
+    down_keep = lax.dynamic_index_in_dim(down_parts, core, 0, keepdims=False)
+    down_send = lax.dynamic_index_in_dim(down_parts, 1 - core, 0, keepdims=False)
+    down_pair = down_keep + swap_core(down_send.astype(BF))
+    down_own = scatter_line(down_pair, line).astype(BF)
+    gu_for = [lax.dynamic_index_in_dim(gu_own, place, 0, keepdims=False) for place in places]
+    gu_mine = natural(
+        [gu_for[0], swap_x(gu_for[1]), swap_y(gu_for[2]), swap_diagonal(gu_for[3])], me
+    )
+
+    upstream = upstream_low.astype(F32)
+    residual_norm_grad, grad_gain_two = pull_norm_two(grad_act_two)
+    grad_residual = upstream + residual_norm_grad
+    residual_back = grad_residual.astype(BF)
+    grad_out = dot_rows(attention, residual_back)
+    attention_back = dot_transposed(residual_back, full_out).astype(BF)
+    attention_back = jnp.transpose(
+        attention_back.reshape(rows, KEY_VALUE_HEADS, group, HEAD_SIZE), (1, 2, 0, 3)
+    ).reshape(KEY_VALUE_HEADS, group * rows, HEAD_SIZE)
+    back_full = attention_back.astype(F32)
+    scaled_back = (back_full / totals).astype(BF)
+    total_back = -jnp.sum(back_full * attended, axis=-1, keepdims=True) / totals
+    through = jnp.einsum("hqd,hkd->hqk", scaled_back, values, preferred_element_type=F32)
+    score_back = (exponent * (through + total_back)).astype(BF)
+    grad_query = by_rows(
+        jnp.einsum("hqk,hkd->hqd", score_back, keys, preferred_element_type=F32) * 0.125
+    )
+    key_part = jnp.einsum("hqk,hqd->hkd", score_back, query, preferred_element_type=F32) * 0.125
+    value_part = jnp.einsum("hqk,hqd->hkd", exponent_low, scaled_back, preferred_element_type=F32)
+    kv_part = jnp.transpose(jnp.stack([key_part, value_part]), (2, 0, 1, 3)).reshape(
+        4 * rows, 2 * kv_width
+    )
+    kv_own = jnp.concatenate(scatter_plane(*token_blocks(kv_part)))
+    turned = jnp.concatenate([grad_query, kv_own[:, :kv_width]], axis=1)
+    turned = pull_rotation(turned.reshape(rows, heads_qk, HEAD_SIZE))[0]
+    linear_back = jnp.concatenate(
+        [turned.reshape(rows, width + kv_width), kv_own[:, kv_width:]], axis=1
+    ).astype(BF)
+    grad_qkv = dot_rows(first_activation, linear_back)
+    grad_act_one = dot_transposed(linear_back, full_qkv)
+    input_norm_grad, grad_gain_one = pull_norm_one(grad_act_one)
+    input_grad = (grad_residual + input_norm_grad)[None]
+
+    def reduce_rows(gradient):
+        columns = gradient.shape[1]
+        parts = gradient.reshape(4, 2, half, columns)
+        keep = lax.dynamic_index_in_dim(parts, core, 1, keepdims=False)
+        send = lax.dynamic_index_in_dim(parts, 1 - core, 1, keepdims=False)
+        pair = keep + swap_core(send.astype(BF))
+        blocks = [
+            halves(lax.dynamic_index_in_dim(pair, place, 0, keepdims=False)) for place in places
+        ]
+        return jnp.concatenate(scatter_plane(*blocks))
+
+    grad_all = jnp.concatenate([reduce_rows(grad_qkv), reduce_rows(grad_out)], axis=1)
+    quarter = grad_all.shape[1] // 4
+    chunks = jnp.transpose(grad_all.reshape(half, 4, quarter), (1, 0, 2))
+    all_own = scatter_line(chunks, line).astype(BF)
+
+    grad_gains = sum_everywhere(jnp.stack([grad_gain_one, grad_gain_two]))
+    squares = (
+        jnp.sum(jnp.square(all_own.astype(F32)))
+        + jnp.sum(jnp.square(gu_mine.astype(F32)))
+        + jnp.sum(jnp.square(down_own.astype(F32)))
+    )
+    total_squares = sum_everywhere(jnp.broadcast_to(squares, (8, 128)))[0, 0]
+    gradient_norm = jnp.sqrt(total_squares + jnp.sum(jnp.square(grad_gains)))
+    clip_factor = jnp.minimum(1.0, jnp.sqrt(F32(PARAMS)) / (gradient_norm + 1e-06))
+
+    def whole(own):
+        ring = jnp.stack(gather_line(own))
+        ring = jnp.concatenate([ring, ring])
+        ordered = lax.dynamic_slice_in_dim(ring, 4 - line, 4, 0)
+        other = swap_core(ordered)
+        first = jnp.where(core == 0, ordered, other)
+        second = jnp.where(core == 0, other, ordered)
+        return jnp.stack([first, second])
+
+    attention_whole = jnp.transpose(whole(all_own), (0, 2, 1, 3)).reshape(shard, 4 * quarter)
+    gu_whole = whole(gu_mine)
+    piece_width = gu_whole.shape[-1]
+    gu_whole = jnp.transpose(
+        gu_whole.reshape(2, 2, 2, 4, half, piece_width), (1, 0, 4, 3, 2, 5)
+    ).reshape(2, shard, 8 * piece_width)
+    down_whole = whole(down_own).reshape(hidden_own, width)
+    own_gains = lax.dynamic_slice_in_dim(grad_gains, me * shard, shard, 1)
+    gradients = (
+        attention_whole[:, :width],
+        attention_whole[:, width : width + kv_width],
+        attention_whole[:, width + kv_width : width + 2 * kv_width],
+        attention_whole[:, width + 2 * kv_width :],
+        gu_whole[0],
+        gu_whole[1],
+        down_whole,
+        own_gains[0],
+        own_gains[1],
+    )
+    momenta = [
+        momentum_beta * moment + clip_factor * gradient
+        for moment, gradient in zip(moments, gradients)
+    ]
+    updated = [
+        master * (1.0 - learning_rate * weight_decay) - learning_rate * momentum
+        for master, momentum in zip(masters, momenta)
+    ]
+    return (output, input_grad, *momenta, *updated, gradient_norm)
+
+
 def solution(mesh):
+    fits = mesh.shape["seq"] == 4 and mesh.shape["dp"] == 8
+    body = fast_device if fits else per_device
     return jax.shard_map(
-        per_device,
+        body,
         mesh=mesh,
         in_specs=(
             P("dp", "seq", None),

time: 1450 us -> 679 us (0.47)
  waiting for transfers between devices: 1090 us -> 131 us
  starting transfers between devices: 0.83 us -> 206 us
  blocking collectives: 122 us -> 0 us
  local copies, waits for them, and re-layouts: 32.4 us -> 131 us
  other arithmetic: 63.3 us -> 99.6 us
  between operations: 24.8 us -> 8.02 us
    reduce_scatter x9 -> x0, waiting for transfers between devices: 645 us -> none  [the longest x1 137 us: per_device(): lax.psum_scatter(grad_up, 'seq', scatter_dimension=0, tiled=True)]
    psum x1 -> x0, waiting for transfers between devices: 246 us -> none  [per_device(): lax.psum((shard_grads[0], shard_grads[1], shard_grads[2], shard_grads[3],...]
    ppermute x0 -> x127, starting transfers between devices: none -> 206 us  [the longest x18 80.9 us: move_up(): return lax.ppermute(value, 'dp', [(i, i + 2) for i in range(6)])]
    all_gather x5 -> x0, waiting for transfers between devices: 198 us -> none  [the longest x1 71.9 us: per_device(): lax.all_gather(shard_up, 'seq', axis=0, tiled=True)]
    ppermute x0 -> x127, waiting for transfers between devices: none -> 131 us  [the longest x36 61.8 us: swap_x(): return lax.ppermute(value, 'seq', [(i, i ^ 1) for i in range(4)])]
    all_gather x4 -> x0, blocking collectives: 69.8 us -> none  [the longest x1 23 us: per_device(): lax.all_gather(key_reduced, 'seq', axis=0, tiled=True)]
    unnamed x2 -> x0, blocking collectives: 27 us -> none
    psum x2 -> x0, blocking collectives: 25.2 us -> none  [the longest x1 14.6 us: per_device(): lax.psum((shard_grads[0], shard_grads[1], shard_grads[2], shard_grads[3],...]
  transfers between devices with their start and end apart: 15 -> 127, of which waited for: 12 -> 41; matrix products, arithmetic and copies ran while one was open for 7% -> 36% of each run, Pallas kernels for 0% -> 0%
where the time goes in v1:
time: 679 us; the launch traced here: 668 us
  starting transfers between devices  206 us (30%)
  local copies, waits for them, and re-layouts  131 us (19%)
  waiting for transfers between devices  131 us (19%)
  other arithmetic  99.6 us (15%)
  matrix products  92.2 us (14%)
  between operations  8.02 us (1%)
    ppermute x18, starting transfers between devices, move_up(): return lax.ppermute(value, 'dp', [(i, i + 2) for i in range(6)])  80.9 us
    ppermute x36, waiting for transfers between devices, swap_x(): return lax.ppermute(value, 'seq', [(i, i ^ 1) for i in range(4)])  61.8 us
    ppermute x36, starting transfers between devices, swap_x(): return lax.ppermute(value, 'seq', [(i, i ^ 1) for i in range(4)])  43.2 us
    ppermute x35, starting transfers between devices, swap_y(): return lax.ppermute(value, 'seq', [(i, i ^ 2) for i in range(4)])  40.5 us
    ppermute x18, waiting for transfers between devices, move_down(): return lax.ppermute(value, 'dp', [(i + 2, i) for i in range(6)])  28.7 us
    ppermute x35, waiting for transfers between devices, swap_y(): return lax.ppermute(value, 'seq', [(i, i ^ 2) for i in range(4)])  26.7 us
    unnamed x217, local copies, waits for them, and re-layouts  26.7 us
    ppermute x18, starting transfers between devices, move_down(): return lax.ppermute(value, 'dp', [(i + 2, i) for i in range(6)])  24.6 us
  transfers between devices with their start and end apart: 127, of which 41 were waited for; matrix products, arithmetic and copies ran while one was open for 36% of the time, Pallas kernels for 0%

profile of v1, /device:TPU:0, one launch (start us, length us, event | category | flops | bytes accessed | tf_op | source)
XLA Modules:
  0.0 668.2 jit_solution(12963634693359867203)
XLA Ops:
  3.2 3.0 collective-permute-start.1
  57.9 3.9 collective-permute-done.3
  70.7 7.8 %collective-permute-done.41 = bf16[128,1152]{1,0:T(8,128)(2,1)S(1)} collective-permute-done((bf16[128,1152]{1,0:T(8,128)(2,1)S(1)}, bf16[128,1152]{1,0:T(8,128)(2,1)S(1)}, u32[]{:S(2)}, u32[]{:S(2)}) %collective-permute-start.41) | collective-permute-done | bytes 294944 | tf_op jit(solution)/shard_map/ppermute | solution.py:413
  87.7 9.0 %collective-permute-done.20 = bf16[72,1152]{1,0:T(8,128)(2,1)S(1)} collective-permute-done((bf16[72,1152]{1,0:T(8,128)(2,1)S(1)}, bf16[72,1152]{1,0:T(8,128)(2,1)S(1)}, u32[]{:S(2)}, u32[]{:S(2)}) %collective-permute-start.20) | collective-permute-done | bytes 165920 | tf_op jit(solution)/shard_map/ppermute | solution.py:413
  101.5 2.8 collective-permute-done.7
  107.1 4.0 collective-permute-done.45
  120.1 3.9 fusion.105
  126.0 3.0 copy.119
  139.3 4.0 collective-permute-done.11
  153.3 3.0 copy.122
  156.6 10.5 %fusion = (f32[6,768]{1,0:T(8,128)S(1)}, f32[6,768,1024]{2,1,0:T(8,128)}) fusion(pred[768,1024]{1,0:T(8,128)(4,1)S(1)} %bitcast.427, bf16[6,768,64]{1,2,0:T(8,128)(2,1)S(1)} %bitcast.410, bf16[2,6,1024,64]{2,3,1,0:T(8,128)(2,1)} %bitcast.401), kind=kOutput, calls=%fused_computation.4 | convolution fusion | flops 618130944 | bytes 21055488 | tf_op jit(solution)/shard_map/hqd,hkd->hqk/dot_general | solution.py:655
  167.1 9.4 %fusion.139 = (bf16[6,768,64]{1,2,0:T(8,128)(2,1)}, f32[6,768,64]{1,2,0:T(8,128)}) fusion(f32[6,768]{1,0:T(8,128)S(1)} %get-tuple-element.151, bf16[2,6,1024,64]{2,3,1,0:T(8,128)(2,1)S(1)} %bitcast.404, f32[6,768,1024]{2,1,0:T(8,128)} %get-tuple-element.152, pred[768,1024]{1,0:T(8,128)(4,1)S(1)} %bitcast.428), kind=kOutput, calls=%fused_computation.414 | convolution fusion | flops 618725376 | bytes 22241280 | tf_op jit(solution)/shard_map/hqk,hkd->hqd/dot_general | solution.py:660
  188.4 6.5 collective-permute-done.24
  197.4 4.9 collective-permute-done.27
  202.4 6.4 fusion.142
  208.8 3.7 fusion.4
  212.6 7.9 %fusion.140 = (bf16[1024,1152]{1,0:T(8,128)(2,1)S(1)}, f32[1024,1152]{1,0:T(8,128)}) fusion(bf16[1152,1536]{1,0:T(8,128)(2,1)} %constant_dynamic-update-slice_fusion.31, bf16[1024,768]{1,0:T(8,128)(2,1)S(1)} %get-tuple-element.58, bf16[1024,768]{1,0:T(8,128)(2,1)S(1)} %get-tuple-element.57), kind=kOutput, calls=%fused_computation.415 | convolution fusion | flops 3631349760 | bytes 13762560 | tf_op jit(solution)/shard_map/dot_general | solution.py:445
  220.4 6.3 fusion.8
  229.0 5.2 fusion.141
  240.2 8.9 %reshape.472 = f32[4,2,144,4,384]{4,3,2,1,0:T(4,128)} reshape(f32[1152,1536]{1,0:T(8,128)} %fusion.8) | data formatting | bytes 14155776 | tf_op jit(solution)/shard_map/reshape | solution.py:691
  250.5 2.8 constant_dynamic-slice_fusion.7
  260.0 5.4 collective-permute-done.36
  269.3 6.1 collective-permute-done.49
  278.4 3.3 collective-permute-done.38
  283.1 4.9 collective-permute-done.37
  292.5 4.3 collective-permute-start.90
  306.4 9.8 %convolution_bitcast_fusion = f32[1,6,1024,64]{2,3,1,0:T(8,128)} fusion(f32[6,768,1024]{2,1,0:T(8,128)} %get-tuple-element.152, pred[768,1024]{1,0:T(8,128)(4,1)S(1)} %bitcast.429, f32[6,768,64]{1,2,0:T(8,128)S(1)} %bitcast.397, f32[6,768]{1,0:T(8,128)S(1)} %copy-done.72), kind=kOutput, calls=%fused_computation.55 | convolution fusion | flops 618725376 | bytes 22431744 | tf_op jit(solution)/shard_map/hqk,hqd->hkd/dot_general | solution.py:724
  316.4 10.2 %multiply_convert_fusion = bf16[6,768,1024]{2,1,0:T(8,128)(2,1)S(1)} fusion(f32[6,768,1024]{2,1,0:T(8,128)} %get-tuple-element.152, f32[6,768]{1,0:T(8,128)S(1)} %negate_divide_fusion, pred[768,1024]{1,0:T(8,128)(4,1)S(1)} %bitcast.430, bf16[2,6,1024,64]{2,3,1,0:T(8,128)(2,1)} %bitcast.402, f32[6,768,64]{1,2,0:T(8,128)} %bitcast.399, f32[6,768]{1,0:T(8,128)S(1)} %copy-done.72), kind=kOutput, calls=%fused_computation.2 | convolution fusion | flops 628162560 | bytes 31100928 | tf_op jit(solution)/shard_map/hqd,hkd->hqk/dot_general | solution.py:718
  326.6 5.2 convolution_multiply_fusion
  372.1 5.3 collective-permute-start.91
  380.2 4.0 fusion.15
  397.6 3.3 collective-permute-start.105
  400.9 3.0 collective-permute-done.94
  403.9 3.2 collective-permute-start.92
  410.7 4.6 collective-permute-start.80
  415.4 3.7 collective-permute-start.121
  421.7 5.2 collective-permute-done.121
  428.2 5.0 collective-permute-start.122
  438.0 4.6 collective-permute-start.81
  442.6 3.9 collective-permute-start.123
  448.3 4.2 collective-permute-done.123
  453.9 6.9 %collective-permute-done.125 = bf16[96,1152]{1,0:T(8,128)(2,1)S(1)} collective-permute-done((bf16[96,1152]{1,0:T(8,128)(2,1)S(1)}, bf16[96,1152]{1,0:T(8,128)(2,1)S(1)}, u32[]{:S(2)}, u32[]{:S(2)}) %collective-permute-start.125) | collective-permute-done | bytes 221216 | tf_op jit(solution)/shard_map/ppermute | solution.py:433
  471.2 7.7 %collective-permute-done.84 = bf16[4,144,384]{2,1,0:T(8,128)(2,1)S(1)} collective-permute-done((bf16[4,144,384]{2,1,0:T(8,128)(2,1)S(1)}, bf16[4,144,384]{2,1,0:T(8,128)(2,1)S(1)}, u32[]{:S(2)}, u32[]{:S(2)}) %collective-permute-start.84) | collective-permute-done | bytes 442400 | tf_op jit(solution)/shard_map/ppermute | solution.py:433
  478.9 3.7 collective-permute-start.82
  486.7 3.0 collective-permute-done.82
  494.2 3.6 collective-permute-start.88
  512.4 5.8 collective-permute-start.114
  526.6 5.4 collective-permute-start.115
  537.2 4.6 collective-permute-start.73
  545.3 4.6 collective-permute-start.116
  551.3 4.6 collective-permute-start.74
  555.9 3.8 collective-permute-done.77
  561.1 4.6 collective-permute-start.75
  576.0 4.4 collective-permute-start.107
  588.0 3.0 collective-permute-start.100
  590.9 4.3 collective-permute-start.108
  600.1 4.6 collective-permute-start.109
  611.4 4.4 collective-permute-done.111
  620.9 3.6 multiply_subtract_fusion
  640.7 4.2 mul.538
  644.9 4.7 copy.146
  649.6 3.9 mul.535
  653.6 8.9 %multiply_subtract_fusion.2 = (f32[288,3072]{1,0:T(8,128)}, f32[288,3072]{1,0:T(8,128)}) fusion(f32[288,3072]{1,0:T(8,128)} %param.28, f32[288,3072]{1,0:T(8,128)} %mul.535, f32[288,3072]{1,0:T(8,128)} %param.37), kind=kLoop, calls=%fused_computation.15 | loop fusion | flops 4423680 | bytes 17694720 | tf_op jit(solution)/shard_map/sub | solution.py:798
  662.5 4.1 multiply_subtract_fusion.1
  (666 shorter events, 336.2 us)
Async XLA Ops:
  3.2 35.4 %collective-permute-start.1 = (bf16[2,288]{1,0:T(2,128)(2,1)}, bf16[2,288]{1,0:T(2,128)(2,1)}, u32[]{:S(2)}, u32[]{:S(2)}) collective-permute-start(bf16[2,288]{1,0:T(2,128)(2,1)} %pad_maximum_fusion.20), channel_id=1, source_target_pairs={{0,16},{8,24},{16,0},{24,8},{1,17},{9,25},{17,1},{25,9},{2,18},{10... | collective-permute-start | bytes 3464 | tf_op jit(solution)/shard_map/ppermute | solution.py:417
  6.1 34.0 %collective-permute-start = (bf16[2,288]{1,0:T(2,128)(2,1)}, bf16[2,288]{1,0:T(2,128)(2,1)}, u32[]{:S(2)}, u32[]{:S(2)}) collective-permute-start(bf16[2,288]{1,0:T(2,128)(2,1)} %pad_maximum_fusion.20), channel_id=1, source_target_pairs={{0,8},{8,0},{16,24},{24,16},{1,9},{9,1},{17,25},{25,17},{2,10},{10... | collective-permute-start | bytes 3464 | tf_op jit(solution)/shard_map/ppermute | solution.py:413
  9.5 76.1 %collective-permute-start.44 = (bf16[128,1152]{1,0:T(8,128)(2,1)}, bf16[128,1152]{1,0:T(8,128)(2,1)}, u32[]{:S(2)}, u32[]{:S(2)}) collective-permute-start(bf16[128,1152]{1,0:T(8,128)(2,1)} %get-tuple-element.135), channel_id=1, source_target_pairs={{0,16},{8,24},{16,0},{24,8},{1,17},{9,25},{17,1},{25,9},{2,18},{10... | collective-permute-start | bytes 884744 | tf_op jit(solution)/shard_map/ppermute | solution.py:417
  10.0 70.0 %collective-permute-start.42 = (bf16[128,1152]{1,0:T(8,128)(2,1)}, bf16[128,1152]{1,0:T(8,128)(2,1)}, u32[]{:S(2)}, u32[]{:S(2)}) collective-permute-start(bf16[128,1152]{1,0:T(8,128)(2,1)} %get-tuple-element.135), channel_id=1, source_target_pairs={{0,8},{8,0},{16,24},{24,16},{1,9},{9,1},{17,25},{25,17},{2,10},{10... | collective-permute-start | bytes 884744 | tf_op jit(solution)/shard_map/ppermute | solution.py:413
  12.3 44.5 %collective-permute-start.19 = (bf16[72,1152]{1,0:T(8,128)(2,1)}, bf16[72,1152]{1,0:T(8,128)(2,1)}, u32[]{:S(2)}, u32[]{:S(2)}) collective-permute-start(bf16[72,1152]{1,0:T(8,128)(2,1)} %get-tuple-element.131), channel_id=1, source_target_pairs={{0,16},{8,24},{16,0},{24,8},{1,17},{9,25},{17,1},{25,9},{2,18},{10... | collective-permute-start | bytes 497672 | tf_op jit(solution)/shard_map/ppermute | solution.py:417
  49.8 20.6 %collective-permute-start.6 = (bf16[72,1920]{1,0:T(8,128)(2,1)}, bf16[72,1920]{1,0:T(8,128)(2,1)S(1)}, u32[]{:S(2)}, u32[]{:S(2)}) collective-permute-start(bf16[72,1920]{1,0:T(8,128)(2,1)} %get-tuple-element.127), channel_id=1, source_target_pairs={{0,16},{8,24},{16,0},{24,8},{1,17},{9,25},{17,1},{25,9},{2,18},{10... | collective-permute-start | bytes 829448 | tf_op jit(solution)/shard_map/ppermute | solution.py:417
  65.0 19.1 %collective-permute-start.43 = (bf16[128,1152]{1,0:T(8,128)(2,1)S(1)}, bf16[128,1152]{1,0:T(8,128)(2,1)S(1)}, u32[]{:S(2)}, u32[]{:S(2)}) collective-permute-start(bf16[128,1152]{1,0:T(8,128)(2,1)S(1)} %copy-done.68), channel_id=1, source_target_pairs={{0,16},{8,24},{16,0},{24,8},{1,17},{9,25},{17,1},{25,9},{2,18},{10... | collective-permute-start | bytes 884744 | tf_op jit(solution)/shard_map/ppermute | solution.py:417
  70.3 29.0 %collective-permute-start.29 = (bf16[144,1536]{1,0:T(8,128)(2,1)S(1)}, bf16[144,1536]{1,0:T(8,128)(2,1)S(1)}, u32[]{:S(2)}, u32[]{:S(2)}) collective-permute-start(bf16[144,1536]{1,0:T(8,128)(2,1)S(1)} %copy-done.63), channel_id=1, source_target_pairs={{0,8},{8,0},{16,24},{24,16},{1,9},{9,1},{17,25},{25,17},{2,10},{10... | collective-permute-start | bytes 1327112 | tf_op jit(solution)/shard_map/ppermute | solution.py:413
  78.5 27.9 %collective-permute-start.31 = (bf16[144,1536]{1,0:T(8,128)(2,1)S(1)}, bf16[144,1536]{1,0:T(8,128)(2,1)S(1)}, u32[]{:S(2)}, u32[]{:S(2)}) collective-permute-start(bf16[144,1536]{1,0:T(8,128)(2,1)S(1)} %pad_maximum_fusion.13), channel_id=1, source_target_pairs={{0,16},{8,24},{16,0},{24,8},{1,17},{9,25},{17,1},{25,9},{2,18},{10... | collective-permute-start | bytes 1327112 | tf_op jit(solution)/shard_map/ppermute | solution.py:417
  80.0 27.0 %collective-permute-start.33 = (bf16[144,1536]{1,0:T(8,128)(2,1)S(1)}, bf16[144,1536]{1,0:T(8,128)(2,1)}, u32[]{:S(2)}, u32[]{:S(2)}) collective-permute-start(bf16[144,1536]{1,0:T(8,128)(2,1)S(1)} %pad_maximum_fusion.14), channel_id=1, source_target_pairs={{0,24},{8,16},{16,8},{24,0},{1,25},{9,17},{17,9},{25,1},{2,26},{10... | collective-permute-start | bytes 1327112 | tf_op jit(solution)/shard_map/ppermute | solution.py:421
  84.2 13.3 %collective-permute-start.21 = (bf16[72,1152]{1,0:T(8,128)(2,1)}, bf16[72,1152]{1,0:T(8,128)(2,1)S(1)}, u32[]{:S(2)}, u32[]{:S(2)}) collective-permute-start(bf16[72,1152]{1,0:T(8,128)(2,1)} %collective-permute-done.17), channel_id=1, source_target_pairs={{0,16},{8,24},{16,0},{24,8},{1,17},{9,25},{17,1},{25,9},{2,18},{10... | collective-permute-start | bytes 497672 | tf_op jit(solution)/shard_map/ppermute | solution.py:417
  85.6 11.0 %collective-permute-start.20 = (bf16[72,1152]{1,0:T(8,128)(2,1)S(1)}, bf16[72,1152]{1,0:T(8,128)(2,1)S(1)}, u32[]{:S(2)}, u32[]{:S(2)}) collective-permute-start(bf16[72,1152]{1,0:T(8,128)(2,1)S(1)} %collective-permute-done.18), channel_id=1, source_target_pairs={{0,8},{8,0},{16,24},{24,16},{1,9},{9,1},{17,25},{25,17},{2,10},{10... | collective-permute-start | bytes 497672 | tf_op jit(solution)/shard_map/ppermute | solution.py:413
  99.4 12.4 %collective-permute-start.46 = (bf16[128,1152]{1,0:T(8,128)(2,1)}, bf16[128,1152]{1,0:T(8,128)(2,1)S(1)}, u32[]{:S(2)}, u32[]{:S(2)}) collective-permute-start(bf16[128,1152]{1,0:T(8,128)(2,1)} %collective-permute-done.42), channel_id=1, source_target_pairs={{0,16},{8,24},{16,0},{24,8},{1,17},{9,25},{17,1},{25,9},{2,18},{10... | collective-permute-start | bytes 884744 | tf_op jit(solution)/shard_map/ppermute | solution.py:417
  111.1 74.6 %collective-permute-start.34 = (bf16[144,1536]{1,0:T(8,128)(2,1)}, bf16[144,1536]{1,0:T(8,128)(2,1)}, u32[]{:S(2)}, u32[]{:S(2)}) collective-permute-start(bf16[144,1536]{1,0:T(8,128)(2,1)} %collective-permute-done.33), channel_id=1, source_target_pairs={{0,1},{1,0},{2,3},{3,2},{4,5},{5,4},{6,7},{7,6},{8,9},{9,8},{10,11... | collective-permute-start | bytes 1327112 | tf_op jit(solution)/shard_map/ppermute | solution.py:425
  134.2 15.8 %collective-permute-start.13 = (bf16[128,768]{1,0:T(8,128)(2,1)S(1)}, bf16[128,768]{1,0:T(8,128)(2,1)S(1)}, u32[]{:S(2)}, u32[]{:S(2)}) collective-permute-start(bf16[128,768]{1,0:T(8,128)(2,1)S(1)} %get-tuple-element.145), channel_id=1, source_target_pairs={{0,16},{8,24},{16,0},{24,8},{1,17},{9,25},{17,1},{25,9},{2,18},{10... | collective-permute-start | bytes 589832 | tf_op jit(solution)/shard_map/ppermute | solution.py:417
  180.6 15.0 %collective-permute-start.25 = (bf16[128,1152]{1,0:T(8,128)(2,1)S(1)}, bf16[128,1152]{1,0:T(8,128)(2,1)S(1)}, u32[]{:S(2)}, u32[]{:S(2)}) collective-permute-start(bf16[128,1152]{1,0:T(8,128)(2,1)S(1)} %get-tuple-element.138), channel_id=1, source_target_pairs={{0,16},{8,24},{16,0},{24,8},{1,17},{9,25},{17,1},{25,9},{2,18},{10... | collective-permute-start | bytes 884744 | tf_op jit(solution)/shard_map/ppermute | solution.py:417
  181.9 15.4 %collective-permute-start.23 = (bf16[128,1152]{1,0:T(8,128)(2,1)S(1)}, bf16[128,1152]{1,0:T(8,128)(2,1)S(1)}, u32[]{:S(2)}, u32[]{:S(2)}) collective-permute-start(bf16[128,1152]{1,0:T(8,128)(2,1)S(1)} %get-tuple-element.138), channel_id=1, source_target_pairs={{0,8},{8,0},{16,24},{24,16},{1,9},{9,1},{17,25},{25,17},{2,10},{10... | collective-permute-start | bytes 884744 | tf_op jit(solution)/shard_map/ppermute | solution.py:413
  183.6 11.3 %collective-permute-start.24 = (bf16[128,1152]{1,0:T(8,128)(2,1)S(1)}, bf16[128,1152]{1,0:T(8,128)(2,1)S(1)}, u32[]{:S(2)}, u32[]{:S(2)}) collective-permute-start(bf16[128,1152]{1,0:T(8,128)(2,1)S(1)} %get-tuple-element.137), channel_id=1, source_target_pairs={{0,8},{8,0},{16,24},{24,16},{1,9},{9,1},{17,25},{25,17},{2,10},{10... | collective-permute-start | bytes 884744 | tf_op jit(solution)/shard_map/ppermute | solution.py:413
  235.2 54.7 %collective-permute-start.89 = (bf16[4,96,1152]{2,1,0:T(8,128)(2,1)}, bf16[4,96,1152]{2,1,0:T(8,128)(2,1)}, u32[]{:S(2)}, u32[]{:S(2)}) collective-permute-start(bf16[4,96,1152]{2,1,0:T(8,128)(2,1)} %fusion.30), channel_id=1, source_target_pairs={{0,1},{1,0},{2,3},{3,2},{4,5},{5,4},{6,7},{7,6},{8,9},{9,8},{10,11... | collective-permute-start | bytes 2654216 | tf_op jit(solution)/shard_map/ppermute | solution.py:425
  236.2 30.7 %collective-permute-start.47 = (bf16[128,1152]{1,0:T(8,128)(2,1)}, bf16[128,1152]{1,0:T(8,128)(2,1)}, u32[]{:S(2)}, u32[]{:S(2)}) collective-permute-start(bf16[128,1152]{1,0:T(8,128)(2,1)} %get-tuple-element.84), channel_id=1, source_target_pairs={{0,8},{8,0},{16,24},{24,16},{1,9},{9,1},{17,25},{25,17},{2,10},{10... | collective-permute-start | bytes 884744 | tf_op jit(solution)/shard_map/ppermute | solution.py:413
  237.9 54.6 %collective-permute-start.52 = (bf16[128,1152]{1,0:T(8,128)(2,1)}, bf16[128,1152]{1,0:T(8,128)(2,1)}, u32[]{:S(2)}, u32[]{:S(2)}) collective-permute-start(bf16[128,1152]{1,0:T(8,128)(2,1)} %get-tuple-element.85), channel_id=1, source_target_pairs={{0,16},{8,24},{16,0},{24,8},{1,17},{9,25},{17,1},{25,9},{2,18},{10... | collective-permute-start | bytes 884744 | tf_op jit(solution)/shard_map/ppermute | solution.py:417
  239.3 29.4 %collective-permute-start.50 = (bf16[128,1152]{1,0:T(8,128)(2,1)}, bf16[128,1152]{1,0:T(8,128)(2,1)}, u32[]{:S(2)}, u32[]{:S(2)}) collective-permute-start(bf16[128,1152]{1,0:T(8,128)(2,1)} %get-tuple-element.86), channel_id=1, source_target_pairs={{0,16},{8,24},{16,0},{24,8},{1,17},{9,25},{17,1},{25,9},{2,18},{10... | collective-permute-start | bytes 884744 | tf_op jit(solution)/shard_map/ppermute | solution.py:417
  239.9 17.2 %collective-permute-start.48 = (bf16[128,1152]{1,0:T(8,128)(2,1)}, bf16[128,1152]{1,0:T(8,128)(2,1)}, u32[]{:S(2)}, u32[]{:S(2)}) collective-permute-start(bf16[128,1152]{1,0:T(8,128)(2,1)} %get-tuple-element.87), channel_id=1, source_target_pairs={{0,8},{8,0},{16,24},{24,16},{1,9},{9,1},{17,25},{25,17},{2,10},{10... | collective-permute-start | bytes 884744 | tf_op jit(solution)/shard_map/ppermute | solution.py:413
  266.9 11.4 %collective-permute-start.35 = (bf16[128,1152]{1,0:T(8,128)(2,1)S(1)}, bf16[128,1152]{1,0:T(8,128)(2,1)S(1)}, u32[]{:S(2)}, u32[]{:S(2)}) collective-permute-start(bf16[128,1152]{1,0:T(8,128)(2,1)S(1)} %get-tuple-element.88), channel_id=1, source_target_pairs={{0,8},{8,0},{16,24},{24,16},{1,9},{9,1},{17,25},{25,17},{2,10},{10... | collective-permute-start | bytes 884744 | tf_op jit(solution)/shard_map/ppermute | solution.py:413
  268.7 13.0 %collective-permute-start.38 = (bf16[128,1152]{1,0:T(8,128)(2,1)S(1)}, bf16[128,1152]{1,0:T(8,128)(2,1)S(1)}, u32[]{:S(2)}, u32[]{:S(2)}) collective-permute-start(bf16[128,1152]{1,0:T(8,128)(2,1)S(1)} %get-tuple-element.90), channel_id=1, source_target_pairs={{0,16},{8,24},{16,0},{24,8},{1,17},{9,25},{17,1},{25,9},{2,18},{10... | collective-permute-start | bytes 884744 | tf_op jit(solution)/shard_map/ppermute | solution.py:417
  275.4 12.6 %collective-permute-start.37 = (bf16[128,1152]{1,0:T(8,128)(2,1)S(1)}, bf16[128,1152]{1,0:T(8,128)(2,1)S(1)}, u32[]{:S(2)}, u32[]{:S(2)}) collective-permute-start(bf16[128,1152]{1,0:T(8,128)(2,1)S(1)} %fusion.51), channel_id=1, source_target_pairs={{0,16},{8,24},{16,0},{24,8},{1,17},{9,25},{17,1},{25,9},{2,18},{10... | collective-permute-start | bytes 884744 | tf_op jit(solution)/shard_map/ppermute | solution.py:417
  278.3 128.9 %collective-permute-start.79 = (bf16[4,144,4,384]{3,1,0,2:T(8,128)(2,1)}, bf16[4,144,4,384]{3,1,0,2:T(8,128)(2,1)}, u32[]{:S(2)}, u32[]{:S(2)}) collective-permute-start(bf16[4,144,4,384]{3,1,0,2:T(8,128)(2,1)} %bitcast.381), channel_id=1, source_target_pairs={{0,1},{1,0},{2,3},{3,2},{4,5},{5,4},{6,7},{7,6},{8,9},{9,8},{10,11... | collective-permute-start | bytes 5308424 | tf_op jit(solution)/shard_map/ppermute | solution.py:425
  281.7 18.2 %collective-permute-start.40 = (bf16[128,1152]{1,0:T(8,128)(2,1)S(1)}, bf16[128,1152]{1,0:T(8,128)(2,1)S(1)}, u32[]{:S(2)}, u32[]{:S(2)}) collective-permute-start(bf16[128,1152]{1,0:T(8,128)(2,1)S(1)} %get-tuple-element.89), channel_id=1, source_target_pairs={{0,16},{8,24},{16,0},{24,8},{1,17},{9,25},{17,1},{25,9},{2,18},{10... | collective-permute-start | bytes 884744 | tf_op jit(solution)/shard_map/ppermute | solution.py:417
  292.5 72.1 %collective-permute-start.90 = (bf16[96,1152]{1,0:T(8,128)(2,1)}, bf16[96,1152]{1,0:T(8,128)(2,1)}, u32[]{:S(2)}, u32[]{:S(2)}) collective-permute-start(bf16[96,1152]{1,0:T(8,128)(2,1)} %get-tuple-element.100), channel_id=1, source_target_pairs={{0,2},{1,3},{2,4},{3,5},{4,6},{5,7},{8,10},{9,11},{10,12},{11,13},... | collective-permute-start | bytes 663560 | tf_op jit(solution)/shard_map/ppermute | solution.py:429
  296.8 97.8 %collective-permute-start.93 = (bf16[96,1152]{1,0:T(8,128)(2,1)}, bf16[96,1152]{1,0:T(8,128)(2,1)}, u32[]{:S(2)}, u32[]{:S(2)}) collective-permute-start(bf16[96,1152]{1,0:T(8,128)(2,1)} %get-tuple-element.101), channel_id=1, source_target_pairs={{2,0},{3,1},{4,2},{5,3},{6,4},{7,5},{10,8},{11,9},{12,10},{13,11},... | collective-permute-start | bytes 663560 | tf_op jit(solution)/shard_map/ppermute | solution.py:433
  350.0 11.8 %collective-permute-start.54 = (bf16[128,768]{1,0:T(8,128)(2,1)S(1)}, bf16[128,768]{1,0:T(8,128)(2,1)}, u32[]{:S(2)}, u32[]{:S(2)}) collective-permute-start(bf16[128,768]{1,0:T(8,128)(2,1)S(1)} %copy.131), channel_id=1, source_target_pairs={{0,8},{8,0},{16,24},{24,16},{1,9},{9,1},{17,25},{25,17},{2,10},{10... | collective-permute-start | bytes 589832 | tf_op jit(solution)/shard_map/ppermute | solution.py:413
  351.7 11.4 %collective-permute-start.56 = (bf16[128,768]{1,0:T(8,128)(2,1)}, bf16[128,768]{1,0:T(8,128)(2,1)}, u32[]{:S(2)}, u32[]{:S(2)}) collective-permute-start(bf16[128,768]{1,0:T(8,128)(2,1)} %copy.133), channel_id=1, source_target_pairs={{0,16},{8,24},{16,0},{24,8},{1,17},{9,25},{17,1},{25,9},{2,18},{10... | collective-permute-start | bytes 589832 | tf_op jit(solution)/shard_map/ppermute | solution.py:417
  368.9 65.8 %collective-permute-start.66 = (bf16[4,144,1152]{2,1,0:T(8,128)(2,1)}, bf16[4,144,1152]{2,1,0:T(8,128)(2,1)}, u32[]{:S(2)}, u32[]{:S(2)}) collective-permute-start(bf16[4,144,1152]{2,1,0:T(8,128)(2,1)} %fusion.13), channel_id=1, source_target_pairs={{0,1},{1,0},{2,3},{3,2},{4,5},{5,4},{6,7},{7,6},{8,9},{9,8},{10,11... | collective-permute-start | bytes 3981320 | tf_op jit(solution)/shard_map/ppermute | solution.py:425
  372.1 22.5 %collective-permute-start.91 = (bf16[96,1152]{1,0:T(8,128)(2,1)}, bf16[96,1152]{1,0:T(8,128)(2,1)}, u32[]{:S(2)}, u32[]{:S(2)}) collective-permute-start(bf16[96,1152]{1,0:T(8,128)(2,1)} %fusion.76), channel_id=1, source_target_pairs={{0,2},{1,3},{2,4},{3,5},{4,6},{5,7},{8,10},{9,11},{10,12},{11,13},... | collective-permute-start | bytes 663560 | tf_op jit(solution)/shard_map/ppermute | solution.py:429
  397.5 85.2 %collective-permute-start.59 = (bf16[4,144,1920]{2,1,0:T(8,128)(2,1)S(1)}, bf16[4,144,1920]{2,1,0:T(8,128)(2,1)S(1)}, u32[]{:S(2)}, u32[]{:S(2)}) collective-permute-start(bf16[4,144,1920]{2,1,0:T(8,128)(2,1)S(1)} %fusion.7), channel_id=1, source_target_pairs={{0,1},{1,0},{2,3},{3,2},{4,5},{5,4},{6,7},{7,6},{8,9},{9,8},{10,11... | collective-permute-start | bytes 6635528 | tf_op jit(solution)/shard_map/ppermute | solution.py:425
  397.6 21.5 %collective-permute-start.105 = (f32[2,1152]{1,0:T(2,128)S(1)}, f32[2,1152]{1,0:T(2,128)S(1)}, u32[]{:S(2)}, u32[]{:S(2)}) collective-permute-start(f32[2,1152]{1,0:T(2,128)S(1)} %add.692), channel_id=1, source_target_pairs={{0,4},{1,5},{2,6},{3,7},{4,0},{5,1},{6,2},{7,3},{8,12},{9,13},{10,... | collective-permute-start | bytes 27656 | tf_op jit(solution)/shard_map/ppermute | solution.py:502
  410.7 22.5 %collective-permute-start.80 = (bf16[4,144,384]{2,1,0:T(8,128)(2,1)S(1)}, bf16[4,144,384]{2,1,0:T(8,128)(2,1)S(1)}, u32[]{:S(2)}, u32[]{:S(2)}) collective-permute-start(bf16[4,144,384]{2,1,0:T(8,128)(2,1)S(1)} %get-tuple-element.74), channel_id=1, source_target_pairs={{0,2},{1,3},{2,4},{3,5},{4,6},{5,7},{8,10},{9,11},{10,12},{11,13},... | collective-permute-start | bytes 1327112 | tf_op jit(solution)/shard_map/ppermute | solution.py:429
  415.4 11.5 %collective-permute-start.121 = (bf16[96,1152]{1,0:T(8,128)(2,1)S(1)}, bf16[96,1152]{1,0:T(8,128)(2,1)S(1)}, u32[]{:S(2)}, u32[]{:S(2)}) collective-permute-start(bf16[96,1152]{1,0:T(8,128)(2,1)S(1)} %get-tuple-element.48), channel_id=1, source_target_pairs={{0,2},{1,3},{2,4},{3,5},{4,6},{5,7},{8,10},{9,11},{10,12},{11,13},... | collective-permute-start | bytes 663560 | tf_op jit(solution)/shard_map/ppermute | solution.py:429
  426.9 34.8 %collective-permute-start.83 = (bf16[4,144,384]{2,1,0:T(8,128)(2,1)S(1)}, bf16[4,144,384]{2,1,0:T(8,128)(2,1)S(1)}, u32[]{:S(2)}, u32[]{:S(2)}) collective-permute-start(bf16[4,144,384]{2,1,0:T(8,128)(2,1)S(1)} %get-tuple-element.75), channel_id=1, source_target_pairs={{2,0},{3,1},{4,2},{5,3},{6,4},{7,5},{10,8},{11,9},{12,10},{13,11},... | collective-permute-start | bytes 1327112 | tf_op jit(solution)/shard_map/ppermute | solution.py:433
  433.3 13.3 %collective-permute-start.124 = (bf16[96,1152]{1,0:T(8,128)(2,1)S(1)}, bf16[96,1152]{1,0:T(8,128)(2,1)S(1)}, u32[]{:S(2)}, u32[]{:S(2)}) collective-permute-start(bf16[96,1152]{1,0:T(8,128)(2,1)S(1)} %collective-permute-done.120), channel_id=1, source_target_pairs={{2,0},{3,1},{4,2},{5,3},{6,4},{7,5},{10,8},{11,9},{12,10},{13,11},... | collective-permute-start | bytes 663560 | tf_op jit(solution)/shard_map/ppermute | solution.py:433
  438.0 25.6 %collective-permute-start.81 = (bf16[4,144,384]{2,1,0:T(8,128)(2,1)S(1)}, bf16[4,144,384]{2,1,0:T(8,128)(2,1)S(1)}, u32[]{:S(2)}, u32[]{:S(2)}) collective-permute-start(bf16[4,144,384]{2,1,0:T(8,128)(2,1)S(1)} %fusion.33), channel_id=1, source_target_pairs={{0,2},{1,3},{2,4},{3,5},{4,6},{5,7},{8,10},{9,11},{10,12},{11,13},... | collective-permute-start | bytes 1327112 | tf_op jit(solution)/shard_map/ppermute | solution.py:429
  446.5 17.5 %collective-permute-start.70 = (bf16[72,1152]{1,0:T(8,128)(2,1)S(1)}, bf16[72,1152]{1,0:T(8,128)(2,1)S(1)}, u32[]{:S(2)}, u32[]{:S(2)}) collective-permute-start(bf16[72,1152]{1,0:T(8,128)(2,1)S(1)} %get-tuple-element.148), channel_id=1, source_target_pairs={{0,16},{8,24},{16,0},{24,8},{1,17},{9,25},{17,1},{25,9},{2,18},{10... | collective-permute-start | bytes 497672 | tf_op jit(solution)/shard_map/ppermute | solution.py:417
  461.7 38.6 %collective-permute-start.72 = (bf16[72,1152]{1,0:T(8,128)(2,1)S(1)}, bf16[72,1152]{1,0:T(8,128)(2,1)S(1)}, u32[]{:S(2)}, u32[]{:S(2)}) collective-permute-start(bf16[72,1152]{1,0:T(8,128)(2,1)S(1)} %get-tuple-element.83), channel_id=1, source_target_pairs={{0,16},{8,24},{16,0},{24,8},{1,17},{9,25},{17,1},{25,9},{2,18},{10... | collective-permute-start | bytes 497672 | tf_op jit(solution)/shard_map/ppermute | solution.py:417
  464.1 57.9 %collective-permute-start.126 = (bf16[4,96,1152]{2,1,0:T(8,128)(2,1)S(1)}, bf16[4,96,1152]{2,1,0:T(8,128)(2,1)}, u32[]{:S(2)}, u32[]{:S(2)}) collective-permute-start(bf16[4,96,1152]{2,1,0:T(8,128)(2,1)S(1)} %constant_dynamic-slice_fusion.3), channel_id=1, source_target_pairs={{0,1},{1,0},{2,3},{3,2},{4,5},{5,4},{6,7},{7,6},{8,9},{9,8},{10,11... | collective-permute-start | bytes 2654216 | tf_op jit(solution)/shard_map/ppermute | solution.py:425
  466.1 12.7 %collective-permute-start.84 = (bf16[4,144,384]{2,1,0:T(8,128)(2,1)S(1)}, bf16[4,144,384]{2,1,0:T(8,128)(2,1)S(1)}, u32[]{:S(2)}, u32[]{:S(2)}) collective-permute-start(bf16[4,144,384]{2,1,0:T(8,128)(2,1)S(1)} %get-tuple-element.73), channel_id=1, source_target_pairs={{2,0},{3,1},{4,2},{5,3},{6,4},{7,5},{10,8},{11,9},{12,10},{13,11},... | collective-permute-start | bytes 1327112 | tf_op jit(solution)/shard_map/ppermute | solution.py:433
  469.8 30.9 %collective-permute-start.71 = (bf16[72,1152]{1,0:T(8,128)(2,1)S(1)}, bf16[72,1152]{1,0:T(8,128)(2,1)S(1)}, u32[]{:S(2)}, u32[]{:S(2)}) collective-permute-start(bf16[72,1152]{1,0:T(8,128)(2,1)S(1)} %get-tuple-element.81), channel_id=1, source_target_pairs={{0,8},{8,0},{16,24},{24,16},{1,9},{9,1},{17,25},{25,17},{2,10},{10... | collective-permute-start | bytes 497672 | tf_op jit(solution)/shard_map/ppermute | solution.py:413
  478.9 10.8 %collective-permute-start.82 = (bf16[4,144,384]{2,1,0:T(8,128)(2,1)S(1)}, bf16[4,144,384]{2,1,0:T(8,128)(2,1)S(1)}, u32[]{:S(2)}, u32[]{:S(2)}) collective-permute-start(bf16[4,144,384]{2,1,0:T(8,128)(2,1)S(1)} %get-tuple-element.72), channel_id=1, source_target_pairs={{0,2},{1,3},{2,4},{3,5},{4,6},{5,7},{8,10},{9,11},{10,12},{11,13},... | collective-permute-start | bytes 1327112 | tf_op jit(solution)/shard_map/ppermute | solution.py:429
  482.7 11.3 %collective-permute-start.85 = (bf16[4,144,384]{2,1,0:T(8,128)(2,1)S(1)}, bf16[4,144,384]{2,1,0:T(8,128)(2,1)S(1)}, u32[]{:S(2)}, u32[]{:S(2)}) collective-permute-start(bf16[4,144,384]{2,1,0:T(8,128)(2,1)S(1)} %fusion.32), channel_id=1, source_target_pairs={{2,0},{3,1},{4,2},{5,3},{6,4},{7,5},{10,8},{11,9},{12,10},{13,11},... | collective-permute-start | bytes 1327112 | tf_op jit(solution)/shard_map/ppermute | solution.py:433
  500.3 10.8 %collective-permute-start.63 = (bf16[72,1920]{1,0:T(8,128)(2,1)}, bf16[72,1920]{1,0:T(8,128)(2,1)}, u32[]{:S(2)}, u32[]{:S(2)}) collective-permute-start(bf16[72,1920]{1,0:T(8,128)(2,1)} %get-tuple-element.140), channel_id=1, source_target_pairs={{0,16},{8,24},{16,0},{24,8},{1,17},{9,25},{17,1},{25,9},{2,18},{10... | collective-permute-start | bytes 829448 | tf_op jit(solution)/shard_map/ppermute | solution.py:417
  500.7 11.7 %collective-permute-start.60 = (bf16[72,1920]{1,0:T(8,128)(2,1)}, bf16[72,1920]{1,0:T(8,128)(2,1)}, u32[]{:S(2)}, u32[]{:S(2)}) collective-permute-start(bf16[72,1920]{1,0:T(8,128)(2,1)} %get-tuple-element.66), channel_id=1, source_target_pairs={{0,8},{8,0},{16,24},{24,16},{1,9},{9,1},{17,25},{25,17},{2,10},{10... | collective-permute-start | bytes 829448 | tf_op jit(solution)/shard_map/ppermute | solution.py:413
  503.9 14.4 %collective-permute-start.62 = (bf16[72,1920]{1,0:T(8,128)(2,1)}, bf16[72,1920]{1,0:T(8,128)(2,1)}, u32[]{:S(2)}, u32[]{:S(2)}) collective-permute-start(bf16[72,1920]{1,0:T(8,128)(2,1)} %fusion.60), channel_id=1, source_target_pairs={{0,16},{8,24},{16,0},{24,8},{1,17},{9,25},{17,1},{25,9},{2,18},{10... | collective-permute-start | bytes 829448 | tf_op jit(solution)/shard_map/ppermute | solution.py:417
  508.6 23.3 %collective-permute-start.65 = (bf16[72,1920]{1,0:T(8,128)(2,1)}, bf16[72,1920]{1,0:T(8,128)(2,1)}, u32[]{:S(2)}, u32[]{:S(2)}) collective-permute-start(bf16[72,1920]{1,0:T(8,128)(2,1)} %get-tuple-element.67), channel_id=1, source_target_pairs={{0,16},{8,24},{16,0},{24,8},{1,17},{9,25},{17,1},{25,9},{2,18},{10... | collective-permute-start | bytes 829448 | tf_op jit(solution)/shard_map/ppermute | solution.py:417
  511.1 14.2 %collective-permute-start.113 = (bf16[4,144,384]{2,1,0:T(8,128)(2,1)S(1)}, bf16[4,144,384]{2,1,0:T(8,128)(2,1)}, u32[]{:S(2)}, u32[]{:S(2)}) collective-permute-start(bf16[4,144,384]{2,1,0:T(8,128)(2,1)S(1)} %gather_fusion.1), channel_id=1, source_target_pairs={{2,0},{3,1},{4,2},{5,3},{6,4},{7,5},{10,8},{11,9},{12,10},{13,11},... | collective-permute-start | bytes 1327112 | tf_op jit(solution)/shard_map/ppermute | solution.py:433
  512.4 14.2 %collective-permute-start.114 = (bf16[4,144,384]{2,1,0:T(8,128)(2,1)S(1)}, bf16[4,144,384]{2,1,0:T(8,128)(2,1)}, u32[]{:S(2)}, u32[]{:S(2)}) collective-permute-start(bf16[4,144,384]{2,1,0:T(8,128)(2,1)S(1)} %gather_fusion.1), channel_id=1, source_target_pairs={{0,2},{1,3},{2,4},{3,5},{4,6},{5,7},{8,10},{9,11},{10,12},{11,13},... | collective-permute-start | bytes 1327112 | tf_op jit(solution)/shard_map/ppermute | solution.py:429
  519.8 12.1 %collective-permute-start.64 = (bf16[72,1920]{1,0:T(8,128)(2,1)S(1)}, bf16[72,1920]{1,0:T(8,128)(2,1)S(1)}, u32[]{:S(2)}, u32[]{:S(2)}) collective-permute-start(bf16[72,1920]{1,0:T(8,128)(2,1)S(1)} %get-tuple-element.65), channel_id=1, source_target_pairs={{0,8},{8,0},{16,24},{24,16},{1,9},{9,1},{17,25},{25,17},{2,10},{10... | collective-permute-start | bytes 829448 | tf_op jit(solution)/shard_map/ppermute | solution.py:413
  525.3 18.5 %collective-permute-start.117 = (bf16[4,144,384]{2,1,0:T(8,128)(2,1)}, bf16[4,144,384]{2,1,0:T(8,128)(2,1)}, u32[]{:S(2)}, u32[]{:S(2)}) collective-permute-start(bf16[4,144,384]{2,1,0:T(8,128)(2,1)} %collective-permute-done.113), channel_id=1, source_target_pairs={{2,0},{3,1},{4,2},{5,3},{6,4},{7,5},{10,8},{11,9},{12,10},{13,11},... | collective-permute-start | bytes 1327112 | tf_op jit(solution)/shard_map/ppermute | solution.py:433
  526.6 18.7 %collective-permute-start.115 = (bf16[4,144,384]{2,1,0:T(8,128)(2,1)}, bf16[4,144,384]{2,1,0:T(8,128)(2,1)}, u32[]{:S(2)}, u32[]{:S(2)}) collective-permute-start(bf16[4,144,384]{2,1,0:T(8,128)(2,1)} %collective-permute-done.114), channel_id=1, source_target_pairs={{0,2},{1,3},{2,4},{3,5},{4,6},{5,7},{8,10},{9,11},{10,12},{11,13},... | collective-permute-start | bytes 1327112 | tf_op jit(solution)/shard_map/ppermute | solution.py:429
  535.1 14.8 %collective-permute-start.76 = (bf16[144,768]{1,0:T(8,128)(2,1)S(1)}, bf16[144,768]{1,0:T(8,128)(2,1)S(1)}, u32[]{:S(2)}, u32[]{:S(2)}) collective-permute-start(bf16[144,768]{1,0:T(8,128)(2,1)S(1)} %bitcast.433), channel_id=1, source_target_pairs={{2,0},{3,1},{4,2},{5,3},{6,4},{7,5},{10,8},{11,9},{12,10},{13,11},... | collective-permute-start | bytes 663560 | tf_op jit(solution)/shard_map/ppermute | solution.py:433
  537.2 14.0 %collective-permute-start.73 = (bf16[144,768]{1,0:T(8,128)(2,1)S(1)}, bf16[144,768]{1,0:T(8,128)(2,1)S(1)}, u32[]{:S(2)}, u32[]{:S(2)}) collective-permute-start(bf16[144,768]{1,0:T(8,128)(2,1)S(1)} %bitcast.432), channel_id=1, source_target_pairs={{0,2},{1,3},{2,4},{3,5},{4,6},{5,7},{8,10},{9,11},{10,12},{11,13},... | collective-permute-start | bytes 663560 | tf_op jit(solution)/shard_map/ppermute | solution.py:429
  543.7 24.6 %collective-permute-start.118 = (bf16[4,144,384]{2,1,0:T(8,128)(2,1)}, bf16[4,144,384]{2,1,0:T(8,128)(2,1)S(1)}, u32[]{:S(2)}, u32[]{:S(2)}) collective-permute-start(bf16[4,144,384]{2,1,0:T(8,128)(2,1)} %collective-permute-done.117), channel_id=1, source_target_pairs={{2,0},{3,1},{4,2},{5,3},{6,4},{7,5},{10,8},{11,9},{12,10},{13,11},... | collective-permute-start | bytes 1327112 | tf_op jit(solution)/shard_map/ppermute | solution.py:433
  545.3 20.3 %collective-permute-start.116 = (bf16[4,144,384]{2,1,0:T(8,128)(2,1)}, bf16[4,144,384]{2,1,0:T(8,128)(2,1)S(1)}, u32[]{:S(2)}, u32[]{:S(2)}) collective-permute-start(bf16[4,144,384]{2,1,0:T(8,128)(2,1)} %collective-permute-done.115), channel_id=1, source_target_pairs={{0,2},{1,3},{2,4},{3,5},{4,6},{5,7},{8,10},{9,11},{10,12},{11,13},... | collective-permute-start | bytes 1327112 | tf_op jit(solution)/shard_map/ppermute | solution.py:429
  576.0 14.9 %collective-permute-start.107 = (bf16[144,768]{1,0:T(8,128)(2,1)}, bf16[144,768]{1,0:T(8,128)(2,1)}, u32[]{:S(2)}, u32[]{:S(2)}) collective-permute-start(bf16[144,768]{1,0:T(8,128)(2,1)} %get-tuple-element.52), channel_id=1, source_target_pairs={{0,2},{1,3},{2,4},{3,5},{4,6},{5,7},{8,10},{9,11},{10,12},{11,13},... | collective-permute-start | bytes 663560 | tf_op jit(solution)/shard_map/ppermute | solution.py:429
  586.6 46.9 %collective-permute-start.119 = (bf16[4,4,144,384]{3,2,1,0:T(8,128)(2,1)}, bf16[4,4,144,384]{3,2,1,0:T(8,128)(2,1)}, u32[]{:S(2)}, u32[]{:S(2)}) collective-permute-start(bf16[4,4,144,384]{3,2,1,0:T(8,128)(2,1)} %constant_dynamic-slice_fusion.4), channel_id=1, source_target_pairs={{0,1},{1,0},{2,3},{3,2},{4,5},{5,4},{6,7},{7,6},{8,9},{9,8},{10,11... | collective-permute-start | bytes 5308424 | tf_op jit(solution)/shard_map/ppermute | solution.py:425
  586.6 12.2 %collective-permute-start.106 = (bf16[144,768]{1,0:T(8,128)(2,1)}, bf16[144,768]{1,0:T(8,128)(2,1)}, u32[]{:S(2)}, u32[]{:S(2)}) collective-permute-start(bf16[144,768]{1,0:T(8,128)(2,1)} %get-tuple-element.52), channel_id=1, source_target_pairs={{2,0},{3,1},{4,2},{5,3},{6,4},{7,5},{10,8},{11,9},{12,10},{13,11},... | collective-permute-start | bytes 663560 | tf_op jit(solution)/shard_map/ppermute | solution.py:433
  (156 other events, 1122.6 us)
